TPU v7x, 256 devices: a whole 4x4x8 slice. The times are simulated.
256 devices in a mesh: row: 32 (over z, y_lo, core), col: 2 (over y_hi), feat: 4 (over x).
Axes of the slice: x: 4, y: 4 (y_hi: 2, y_lo: 2; y = y_hi * 2 + y_lo), z: 8, core: 2. Of those that a mesh axis runs over, the one named last changes fastest.
Arguments:
- cotangent: bfloat16 [256, 65536], P('feat', ('row', 'col')), may hold values from -6 to 6
- preact: bfloat16 [256, 65536], P('feat', ('row', 'col')), may hold values from -6 to 6
- features: bfloat16 [256, 65536], P(None, ('row', 'col')), may hold values from -6 to 6
- aggregated: bfloat16 [256, 65536], P(None, ('row', 'col')), may hold values from -6 to 6
- w_self: bfloat16 [256, 256], replicated, may hold values from -0.375 to 0.375
- w_neigh: bfloat16 [256, 256], replicated, may hold values from -0.375 to 0.375
- tile_rows: int32 [16384], P(('row', 'col')), may hold values from 0 to 511, as said below
- tile_cols: int32 [16384], P(('row', 'col')), may hold values from 0 to 511, as said below
- tile_vals: bfloat16 [16384, 128, 128], P(('row', 'col')), may hold values from -0.09375 to 0.09375
- tile_live: int32 [64], P(('row', 'col')), may hold values from 1 to 256, as said below
Outputs:
- input_grad: bfloat16 [256, 65536], P('feat', ('row', 'col'))
- grad_self: float32 [256, 256], P(None, 'feat')
- grad_neigh: float32 [256, 256], P(None, 'feat')
Inputs may be any that keep to these rules, and one draw needn't show every extreme that they name: `tile_rows`: slot s lies in group g = s // 256, g = r * 2 + c; its row block lies among the 2 * 8 blocks from r * 2 * 8 onward. Several slots may name the same block pair. `tile_cols`: with g = r * 2 + c as above, the column block of slot s is q * 2 * 8 + c * 8 + u for some q < 32 and u < 8. `tile_live`: some group has all 256 slots live in every draw.
All inputs are finite; a program needn't handle non-finite values.
Results may differ from a plain program's by a relative error of at most 0.0033.
Values may be sent and summed in bfloat16 or wider, within the bound.
No kernel may reach another device: no remote copies, remote signals or barrier semaphores. Data moves between devices by JAX's collectives and lax.ppermute only.
A program may use at most 128 MiB of HBM per device.

v0:
```python
import jax
import jax.numpy as jnp
from jax import lax
from jax.sharding import PartitionSpec as P


def contract_nodes(left, right):
    return lax.dot_general(
        left, right, (((1,), (1,)), ((), ())), preferred_element_type=jnp.float32
    )


def tile_products(panel_blocks, local_rows, values, keep_mask):
    pieces = panel_blocks[local_rows]
    products = jnp.einsum("sfi,sij->sfj", pieces, values, preferred_element_type=jnp.float32)
    return products * keep_mask[:, None, None]


def on_device(
    cotangent,
    preact,
    features,
    aggregated,
    w_self,
    w_neigh,
    tile_rows,
    tile_cols,
    tile_vals,
    tile_live,
):
    delta = jnp.where(preact > 0, cotangent, jnp.zeros_like(cotangent))
    node_cnt = delta.shape[1]
    in_width = w_self.shape[0]
    in_rows = in_width // lax.axis_size("feat")
    feat_pos = lax.axis_index("feat")
    grad_self, grad_neigh = lax.psum(
        (contract_nodes(features, delta), contract_nodes(aggregated, delta)), ("row", "col")
    )
    gathered = lax.all_gather(delta, "feat", axis=0, tiled=True)
    neigh_rows = lax.dynamic_slice_in_dim(w_neigh, feat_pos * in_rows, in_rows, 0)
    self_rows = lax.dynamic_slice_in_dim(w_self, feat_pos * in_rows, in_rows, 0)
    propagated = jnp.dot(neigh_rows, gathered, preferred_element_type=jnp.float32)
    self_term = jnp.dot(self_rows, gathered, preferred_element_type=jnp.float32)
    panel = lax.all_gather(propagated.astype(jnp.bfloat16), "col", axis=1, tiled=True)
    n_row = lax.axis_size("row")
    n_col = lax.axis_size("col")
    row_pos = lax.axis_index("row")
    col_span = node_cnt // 128
    row_span = n_col * col_span
    local_rows = tile_rows - row_pos * row_span
    target = tile_cols // row_span * col_span + tile_cols % col_span
    panel_blocks = panel.reshape(in_rows, row_span, 128).transpose(1, 0, 2)
    slots = tile_vals.shape[0]
    live_count = tile_live[0]
    empty = jnp.zeros((n_row * col_span, in_rows, 128), jnp.float32)
    keep_mask = (jnp.arange(slots) < live_count).astype(jnp.float32)
    totals = empty.at[target].add(tile_products(panel_blocks, local_rows, tile_vals, keep_mask))
    reduced = lax.psum_scatter(totals, "row", scatter_dimension=0, tiled=True)
    summed = reduced.transpose(1, 0, 2).reshape(in_rows, node_cnt)
    input_grad = (summed + self_term).astype(jnp.bfloat16)
    return (input_grad, grad_self, grad_neigh)


def solution(mesh):
    return jax.shard_map(
        on_device,
        mesh=mesh,
        in_specs=(
            P("feat", ("row", "col")),
            P("feat", ("row", "col")),
            P(None, ("row", "col")),
            P(None, ("row", "col")),
            P(),
            P(),
            P(("row", "col")),
            P(("row", "col")),
            P(("row", "col"), None, None),
            P(("row", "col")),
        ),
        out_specs=(P("feat", ("row", "col")), P(None, "feat"), P(None, "feat")),
        check_vma=False,
    )
```

profile of v0, /device:TPU:1, one launch (start us, length us, event | category | flops | bytes accessed | tf_op | source)
XLA Modules:
  0.0 284.4 jit_solution(15233211726554660374)
XLA Ops:
  8.0 0.0 copy-start
  8.0 0.0 reduce-scatter.2.cloned.1.call-start
  8.8 0.7 compare_select_fusion.2
  9.5 0.7 compare_select_fusion.1
  10.2 1.0 compare_select_fusion
  11.1 12.3 %all_gather.6 = bf16[256,1024]{1,0:T(8,128)(2,1)S(1)} all-gather(bf16[64,1024]{1,0:T(8,128)(2,1)S(1)} %compare_select_fusion), channel_id=1, replica_groups=mesh['row'=32,'col'=2,'feat'=4] {'feat'}, dimensions={0}, use_global_device_ids=true | all-gather | bytes 655360 | tf_op jit(solution)/shard_map/all_gather | solution.py:39
  23.5 1.0 convolution_convert_fusion
  24.5 6.0 %all_gather.7 = bf16[64,2048]{1,0:T(8,128)(2,1)S(1)} all-gather(bf16[64,1024]{1,0:T(8,128)(2,1)S(1)} %convolution_convert_fusion), channel_id=1, replica_groups=mesh['row'=32,'col'=2,'feat'=4] {'col'}, dimensions={1}, use_global_device_ids=true | all-gather | bytes 393216 | tf_op jit(solution)/shard_map/all_gather | solution.py:44
  30.5 0.1 bitcast_bitcast_fusion
  30.5 3.1 %gather_fusion = bf16[256,64,128]{2,1,0:T(8,128)(2,1)} fusion(bf16[16,64,128]{2,1,0:T(8,128)(2,1)S(1)} %bitcast_bitcast_fusion, s32[1024]{0:T(1024)S(1)} %pad_clamp_fusion), kind=kCustom, calls=%fused_computation | custom fusion | bytes 8389632 | tf_op jit(solution)/shard_map/gather | solution.py:14
  33.6 10.2 %broadcast_multiply_fusion = f32[256,64,128]{2,1,0:T(8,128)} fusion(f32[256]{0:T(256)S(1)} %compare_convert_fusion, bf16[256,64,128]{2,1,0:T(8,128)(2,1)} %gather_fusion, bf16[256,128,128]{2,1,0:T(8,128)(2,1)} %param.18), kind=kOutput, calls=%fused_computation.2 | convolution fusion | flops 538968064 | bytes 20972544 | tf_op jit(solution)/shard_map/sfi,sij->sfj/dot_general | solution.py:15
  43.8 4.3 %broadcast_in_dim.10 = f32[256,64,128]{2,1,0:T(8,128)} broadcast(f32[]{:T(128)} %constant.21.clone.1), dimensions={} | broadcast | bytes 8388612 | tf_op jit(solution)/shard_map/broadcast_in_dim | solution.py:55
  48.0 39.4 %scatter_fusion = f32[256,64,128]{2,1,0:T(8,128)} fusion(f32[256,64,128]{2,1,0:T(8,128)} %broadcast_in_dim.10, s32[256]{0:T(256)S(1)} %compare_select_fusion.2, f32[256,64,128]{2,1,0:T(8,128)} %broadcast_multiply_fusion), kind=kCustom, calls=%fused_computation.1 | custom fusion | flops 2097152 | bytes 25166848 | tf_op jit(solution)/shard_map/scatter-add | solution.py:57
  87.4 0.0 copy-start.1
  87.4 0.0 reduce-scatter.2.cloned.1.call-update
  87.5 0.0 all-reduce.3.cloned.1.call-start
  87.5 0.0 copy-done
  87.5 0.9 convolution_bitcast_fusion
  88.4 0.0 copy-done.1
  88.5 0.9 convolution_bitcast_fusion.1
  89.4 0.0 all-reduce.3.cloned.1.call-update
  89.4 131.1 %reduce-scatter.2.cloned.1.call-done = f32[8,64,128]{2,1,0:T(8,128)} async-done(((f32[256,64,128]{2,1,0:T(8,128)}), f32[8,64,128]{2,1,0:T(8,128)}) %reduce-scatter.2.cloned.1.call-update) | async-done | bytes 262160 | tf_op jit(solution)/shard_map/reduce_scatter | solution.py:58
  220.5 1.8 fusion
  222.4 51.6 %all-reduce.3.cloned.1.call-done = (f32[256,64]{0,1:T(8,128)}, f32[256,64]{0,1:T(8,128)}) async-done(((f32[256,64]{0,1:T(8,128)}, f32[256,64]{0,1:T(8,128)}), (f32[256,64]{0,1:T(8,128)}, f32[256,64]{0,1:T(8,128)})) %all-reduce.3.cloned.1.call-update) | async-done | bytes 131088 | tf_op jit(solution)/shard_map/psum | solution.py:36
  274.0 1.5 copy.23
  275.4 1.5 copy.24
  (2 shorter events, 0.0 us)
Async XLA Ops:
  8.0 79.5 %copy-start = (bf16[256,1024]{1,0:T(8,128)(2,1)S(1)}, bf16[256,1024]{1,0:T(8,128)(2,1)}, u32[]{:S(2)}) copy-start(bf16[256,1024]{1,0:T(8,128)(2,1)} %param.13) | copy-start | bytes 1572868
  8.0 212.5 %reduce-scatter.2.cloned.1.call-start = ((), (), s32[]{:S(2)}) async-start(), calls=%async_computation.1 | async-start | bytes 8650752 | tf_op jit(solution)/shard_map/reduce_scatter | solution.py:58
  87.4 1.0 copy-start.1
  87.5 186.5 %all-reduce.3.cloned.1.call-start = ((), (), s32[]{:S(2)}) async-start(), calls=%async_computation.2 | async-start | bytes 262144 | tf_op jit(solution)/shard_map/psum | solution.py:36
Sparse Core Ops, SparseCore 0:
  87.6 132.8 reduce-scatter.1
Sparse Core Ops, SparseCore 1:
  92.1 181.9 all-reduce.2
where the time goes:
time: 285 us; the launch traced here: 284 us
  waiting for transfers between devices  183 us (64%)
  other arithmetic  41.8 us (15%)
  blocking collectives  18.3 us (6%)
  between operations  16.2 us (6%)
  matrix products  14.8 us (5%)
  local copies, waits for them, and re-layouts  10.4 us (4%)
    reduce_scatter x1, waiting for transfers between devices, on_device(): reduced = lax.psum_scatter(totals, 'row', scatter_dimension=0, tiled=True)  131 us
    psum x1, waiting for transfers between devices, on_device(): lax.psum((contract_nodes(features, delta), contract_nodes(aggregated, del...  51.6 us
    scatter-add x1, other arithmetic, on_device(): empty.at[target]  39.4 us
    all_gather x1, blocking collectives, on_device(): gathered = lax.all_gather(delta, 'feat', axis=0, tiled=True)  12.3 us
    dot_general x1, matrix products, tile_products(): jnp.einsum('sfi,sij->sfj', pieces, values, preferred_element_type=jnp.flo...  10.2 us
    all_gather x1, blocking collectives, on_device(): lax.all_gather(propagated.astype(jnp.bfloat16), 'col', axis=1, tiled=True)  6 us
  transfers between devices with their start and end apart: 2, of which 2 were waited for; matrix products, arithmetic and copies ran while one was open for 1% of the time, Pallas kernels for 0%

commit v1 on v0

v1 whole, which is shorter than its diff:
```python
import jax
import jax.numpy as jnp
from jax import lax
from jax.experimental import pallas as pl
from jax.experimental.pallas import tpu as pltpu
from jax.sharding import Mesh, PartitionSpec as P

AXES = ("z", "pair", "core", "half", "x")
BLOCK = 128
GROUP = 8
DEPTH = 4
ROOM = 256 + GROUP


def swap(n):
    return [(i, i ^ 1) for i in range(n)]


def turn(k, n):
    return [(i, (i + k) % n) for i in range(n)]


EVEN_PAIRS = swap(8)
ODD_PAIRS = [(i, (((i + 1) % 8 ^ 1) - 1) % 8) for i in range(8)]


def list_kernel(live_ref, entry_ref, mine_ref, lists_ref, count_ref):
    def place(slot, counts):
        other, own = counts
        mine = mine_ref[slot]
        lists_ref[jnp.where(mine == 1, ROOM + own, other)] = entry_ref[slot]
        return other + 1 - mine, own + mine

    other, own = lax.fori_loop(0, live_ref[0], place, (jnp.int32(0), jnp.int32(0)))
    for k in range(GROUP):
        lists_ref[other + k] = jnp.int32(BLOCK)
        lists_ref[ROOM + own + k] = jnp.int32(BLOCK)
    count_ref[0] = other
    count_ref[1] = own


def make_lists(live, entries, mine):
    smem = pl.BlockSpec(memory_space=pltpu.SMEM)
    return pl.pallas_call(
        list_kernel,
        out_shape=(jax.ShapeDtypeStruct((2 * ROOM,), jnp.int32), jax.ShapeDtypeStruct((2,), jnp.int32)),
        in_specs=[smem] * 3,
        out_specs=(smem, smem),
    )(live, entries, mine)


def tile_kernel(which, lists_ref, count_ref, near_ref, far_ref, vals_ref, out_ref, total, panel, tiles, sems):
    base = which * ROOM
    steps = (count_ref[which] + GROUP - 1) // GROUP

    def fetch(step):
        slot = lax.rem(step, DEPTH)
        for k in range(GROUP):
            entry = lists_ref[base + step * GROUP + k]
            pltpu.make_async_copy(
                vals_ref.at[lax.shift_right_logical(entry, 16)], tiles.at[slot * GROUP + k], sems.at[slot]
            ).start()

    for s in range(DEPTH - 1):
        pl.when(s < steps)(lambda s=s: fetch(jnp.int32(s)))
    panel[0:8] = near_ref[...]
    panel[8:16] = far_ref[...]
    total[...] = jnp.zeros_like(total)

    def body(step, carry):
        slot = lax.rem(step, DEPTH)
        pl.when(step + DEPTH - 1 < steps)(lambda: fetch(step + DEPTH - 1))
        held = tiles.at[pl.ds(slot * GROUP, GROUP)]
        pltpu.make_async_copy(vals_ref.at[pl.ds(0, GROUP)], held, sems.at[slot]).wait()
        places, products = [], []
        for k in range(GROUP):
            entry = lists_ref[base + step * GROUP + k]
            block = lax.shift_right_logical(entry, 8) & 255
            places.append(entry & 255)
            products.append(jnp.dot(panel[block], held[k], preferred_element_type=jnp.float32))
        for place, product in zip(places, products):
            total[place] += product
        return carry

    lax.fori_loop(0, steps, body, 0)
    out_ref[...] = total[0:BLOCK].astype(out_ref.dtype)


def tile_sums(which, lists, counts, near, far, vals, dtype):
    rows = near.shape[1]
    smem = pl.BlockSpec(memory_space=pltpu.SMEM)
    vmem = pl.BlockSpec(memory_space=pltpu.VMEM)
    return pl.pallas_call(
        lambda *refs: tile_kernel(which, *refs),
        out_shape=jax.ShapeDtypeStruct((BLOCK, rows, BLOCK), dtype),
        in_specs=[smem, smem, vmem, vmem, pl.BlockSpec(memory_space=pl.ANY)],
        out_specs=vmem,
        scratch_shapes=[
            pltpu.VMEM((BLOCK + 1, rows, BLOCK), jnp.float32),
            pltpu.VMEM((16, rows, BLOCK), jnp.bfloat16),
            pltpu.VMEM((DEPTH * GROUP, BLOCK, BLOCK), jnp.bfloat16),
            pltpu.SemaphoreType.DMA((DEPTH,)),
        ],
        compiler_params=pltpu.CompilerParams(vmem_limit_bytes=24 * 1024 * 1024),
        cost_estimate=pl.CostEstimate(flops=2 * 128 * rows * 128 * 128, bytes_accessed=8 << 20, transcendentals=0),
    )(lists, counts, near, far, vals)


def half16(x):
    return x.astype(jnp.bfloat16)


def wide(x):
    return x.astype(jnp.float32)


def reduce_blocks(keep):
    first, second, third, fourth = (keep[32 * g : 32 * g + 32].reshape(2, 2, 4, 2, *keep.shape[1:]) for g in range(4))
    came_first = lax.ppermute(half16(first[1]), "z", EVEN_PAIRS)
    came_second = lax.ppermute(half16(second[1]), "z", ODD_PAIRS)
    late = jnp.concatenate([third, fourth], axis=3)
    came_late = lax.ppermute(half16(late[1]), "pair", swap(2))
    early = jnp.concatenate([first[0] + wide(came_first), second[0] + wide(came_second)], axis=2)
    late = late[0] + wide(came_late)
    came_early = lax.ppermute(half16(early[1]), "pair", swap(2))
    came_third = lax.ppermute(half16(late[1, :, :2]), "z", EVEN_PAIRS)
    came_fourth = lax.ppermute(half16(late[1, :, 2:]), "z", ODD_PAIRS)
    early = early[0] + wide(came_early)
    late = jnp.concatenate([late[0, :, :2] + wide(came_third), late[0, :, 2:] + wide(came_fourth)], axis=1)
    both = jnp.concatenate([early, late], axis=1)
    rounded = half16(both)
    total = both[0]
    for k in (1, 3, 2):
        total = total + wide(lax.ppermute(rounded[k], "z", turn(2 * k, 8)))
    return total


def reduce_weights(grads):
    halves = (("core", lax.axis_index("core")), ("pair", lax.axis_index("pair")), ("half", lax.axis_index("half")))
    part = grads
    for axis, me in halves:
        n = part.shape[0] // 2
        mine = lax.dynamic_slice_in_dim(part, me * n, n, 0)
        other = lax.dynamic_slice_in_dim(part, (1 - me) * n, n, 0)
        part = mine + lax.ppermute(other, axis, swap(2))
    for k in (1, 2, 4):
        part = part + lax.ppermute(part, "z", [(i, i ^ k) for i in range(8)])
    for axis, me in reversed(halves):
        came = lax.ppermute(part, axis, swap(2))
        part = jnp.where(me == 0, jnp.concatenate([part, came]), jnp.concatenate([came, part]))
    return part


def contract_nodes(left, right):
    return lax.dot_general(left, right, (((1,), (1,)), ((), ())), preferred_element_type=jnp.float32)


def on_device(
    cotangent, preact, features, aggregated, w_self, w_neigh, tile_rows, tile_cols, tile_vals, tile_live
):
    z, pair, core, half, x = (lax.axis_index(a) for a in AXES)
    delta = jnp.where(preact > 0, cotangent, jnp.zeros_like(cotangent))
    rows, nodes = delta.shape
    in_width = w_self.shape[0]

    grads = reduce_weights(
        jnp.concatenate([contract_nodes(features, delta), contract_nodes(aggregated, delta)], axis=0)
    )

    hidden = [delta] + [lax.ppermute(delta, "x", turn(k, 4)) for k in (1, 2, 3)]
    weights = jnp.concatenate(
        [lax.dynamic_slice_in_dim(w, x * rows, rows, 0) for w in (w_neigh, w_self)], axis=0
    )
    weights = jnp.concatenate(
        [lax.dynamic_slice_in_dim(weights, (x + 4 - k) % 4 * rows, rows, 1) for k in range(4)], axis=1
    )
    both = jnp.dot(weights, jnp.concatenate(hidden, axis=0), preferred_element_type=jnp.float32)
    near = half16(both[:rows]).reshape(rows, nodes // BLOCK, BLOCK).transpose(1, 0, 2)
    far = lax.ppermute(near, "half", swap(2))
    self_term = both[rows:]

    slots = jnp.arange(tile_rows.shape[0], dtype=jnp.int32)
    owner, within = tile_cols // 16, tile_cols % 8
    group = within // 2
    shift = group % 2
    at, me = (owner // 4 + shift) % 8, (z + shift) % 8
    step = (at % 2) ^ (me % 2)
    turns = (at // 2 - me // 2 + 4) % 4
    across = (owner // 2 % 2) ^ pair
    outer = jnp.where(group < 2, step, across)
    inner = jnp.where(group < 2, across, step)
    place = group * 32 + ((outer * 2 + inner) * 4 + turns) * 2 + within % 2
    block = (tile_rows - (z * 4 + pair * 2 + core) * 16) ^ (half * 8)
    lists, counts = make_lists(
        tile_live, slots * 65536 + block * 256 + place, 1 - ((owner % 2) ^ core).astype(jnp.int32)
    )

    away = tile_sums(0, lists, counts, near, far, tile_vals, jnp.bfloat16)
    came = lax.ppermute(away, "core", swap(2))
    keep = tile_sums(1, lists, counts, near, far, tile_vals, jnp.float32)
    summed = reduce_blocks(keep + wide(came))
    summed = summed.transpose(1, 0, 2).reshape(rows, nodes)
    input_grad = half16(summed + self_term)
    return (input_grad, grads[:in_width], grads[in_width:])


def solution(mesh):
    nodes = ("z", "pair", "core", "half")
    return jax.shard_map(
        on_device,
        mesh=Mesh(mesh.devices.reshape(8, 2, 2, 2, 4), AXES),
        in_specs=(
            P("x", nodes),
            P("x", nodes),
            P(None, nodes),
            P(None, nodes),
            P(),
            P(),
            P(nodes),
            P(nodes),
            P(nodes, None, None),
            P(nodes),
        ),
        out_specs=(P("x", nodes), P(None, "x"), P(None, "x")),
        check_vma=False,
    )
```

time: 285 us -> 140 us (0.49)
  the two profiles are of different devices: /device:TPU:1 before, /device:TPU:16 now
where the time goes in v1:
time: 140 us; the launch traced here: 139 us
  waiting for transfers between devices  59 us (42%)
  starting transfers between devices  53.6 us (38%)
  local copies, waits for them, and re-layouts  9.96 us (7%)
  other arithmetic  6.9 us (5%)
  Pallas kernels  6.74 us (5%)
  between operations  1.66 us (1%)
    ppermute x1, starting transfers between devices, reduce_blocks(): came_second = lax.ppermute(half16(second[1]), 'z', ODD_PAIRS)  15.1 us
    ppermute x3, starting transfers between devices, reduce_weights(): part = part + lax.ppermute(part, 'z', [(i, i ^ k) for i in range(8)])  14.4 us
    ppermute x3, waiting for transfers between devices, reduce_weights(): part = mine + lax.ppermute(other, axis, swap(2))  10.7 us
    ppermute x3, starting transfers between devices, reduce_blocks(): total = total + wide(lax.ppermute(rounded[k], 'z', turn(2 * k, 8)))  10 us
    ppermute x1, waiting for transfers between devices, reduce_blocks(): came_late = lax.ppermute(half16(late[1]), 'pair', swap(2))  10 us
    ppermute x3, waiting for transfers between devices, reduce_weights(): came = lax.ppermute(part, axis, swap(2))  8.37 us
    unnamed x20, local copies, waits for them, and re-layouts  8.09 us
    ppermute x3, waiting for transfers between devices, reduce_weights(): part = part + lax.ppermute(part, 'z', [(i, i ^ k) for i in range(8)])  6.49 us
  transfers between devices with their start and end apart: 23, of which 18 were waited for; matrix products, arithmetic and copies ran while one was open for 3% of the time, Pallas kernels for 3%

profile of v1, /device:TPU:16, one launch (start us, length us, event | category | flops | bytes accessed | tf_op | source)
XLA Modules:
  0.0 138.7 jit_solution(2325711607939999487)
XLA Ops:
  0.6 1.0 compare_select_fusion
  1.7 2.8 %collective-permute-start.2 = (bf16[64,1024]{1,0:T(8,128)(2,1)S(1)}, bf16[64,1024]{1,0:T(8,128)(2,1)S(1)}, u32[]{:S(2)}, u32[]{:S(2)}) collective-permute-start(bf16[64,1024]{1,0:T(8,128)(2,1)S(1)} %compare_select_fusion), channel_id=1, source_target_pairs={{0,3},{1,0},{2,1},{3,2},{4,7},{5,4},{6,5},{7,6},{8,11},{9,8},{10,9... | collective-permute-start | bytes 393224 | tf_op jit(solution)/shard_map/ppermute | solution.py:170
  4.5 0.8 collective-permute-start.1
  5.3 0.9 collective-permute-start
  6.2 1.3 fusion.52
  7.5 0.8 constant_dynamic-slice_fusion.2
  9.0 1.5 %shard_map.121 = (s32[528]{0:T(1024)}, s32[2]{0:T(128)}) custom-call(s32[1]{0:T(128)S(6)} %copy.20.live_ref, s32[256]{0:T(256)} %get-tuple-element.31.entry_ref, s32[256]{0:T(256)} %get-tuple-element.30.mine_ref), custom_call_target="tpu_custom_call" | custom-call | tf_op jit(solution)/shard_map/pallas_call | solution.py:44
  10.5 0.1 fusion.37
  10.6 1.8 %collective-permute-done.1 = bf16[64,1024]{1,0:T(8,128)(2,1)S(1)} collective-permute-done((bf16[64,1024]{1,0:T(8,128)(2,1)S(1)}, bf16[64,1024]{1,0:T(8,128)(2,1)S(1)}, u32[]{:S(2)}, u32[]{:S(2)}) %collective-permute-start.1) | collective-permute-done | bytes 131104 | tf_op jit(solution)/shard_map/ppermute | solution.py:170
  12.4 1.4 %collective-permute-done = bf16[64,1024]{1,0:T(8,128)(2,1)S(1)} collective-permute-done((bf16[64,1024]{1,0:T(8,128)(2,1)S(1)}, bf16[64,1024]{1,0:T(8,128)(2,1)S(1)}, u32[]{:S(2)}, u32[]{:S(2)}) %collective-permute-start) | collective-permute-done | bytes 131104 | tf_op jit(solution)/shard_map/ppermute | solution.py:170
  13.8 0.3 fusion.9
  14.1 0.4 collective-permute-start.3
  14.5 0.3 convolution_bitcast_fusion
  14.8 6.1 %collective-permute-done.3.refs_3_ = bf16[8,64,128]{2,1,0:T(8,128)(2,1)S(1)} collective-permute-done((bf16[8,64,128]{2,1,0:T(8,128)(2,1)S(1)}, bf16[8,64,128]{2,1,0:T(8,128)(2,1)S(1)}, u32[]{:S(2)}, u32[]{:S(2)}) %collective-permute-start.3) | collective-permute-done | bytes 131104 | tf_op jit(solution)/shard_map/ppermute | solution.py:179
  20.9 3.4 %copy-done.1 = bf16[256,128,128]{2,1,0:T(8,128)(2,1)S(1)} copy-done((bf16[256,128,128]{2,1,0:T(8,128)(2,1)S(1)}, bf16[256,128,128]{2,1,0:T(8,128)(2,1)}, u32[]{:S(2)}) %copy-start.1) | copy-done | bytes 8388632
  24.3 0.7 copy-done.3
  25.0 0.6 copy-done.5
  25.6 2.9 %shard_map.123 = bf16[128,64,128]{2,1,0:T(8,128)(2,1)S(1)} custom-call(s32[528]{0:T(1024)S(1)} %copy-done.3, s32[2]{0:T(128)S(1)} %copy-done.5, bf16[8,64,128]{2,1,0:T(8,128)(2,1)S(1)} %bitcast_bitcast_fusion.refs_2_, bf16[8,64,128]{2,1,0:T(8,128)(2,1)S(1)} %collective-permute-done.3.refs_3_, bf16[256,128,128]{2,1,0:T(8,128)(2,1)S(1)} %copy-done.1), custom_call_target="tpu_custom_call" | custom-call | flops 268435456 | bytes 8388608 | tf_op jit(solution)/shard_map/pallas_call | solution.py:93
  28.5 2.5 %collective-permute-start.4 = (bf16[128,64,128]{2,1,0:T(8,128)(2,1)S(1)}, bf16[128,64,128]{2,1,0:T(8,128)(2,1)}, u32[]{:S(2)}, u32[]{:S(2)}) collective-permute-start(bf16[128,64,128]{2,1,0:T(8,128)(2,1)S(1)} %shard_map.123), channel_id=1, source_target_pairs={{0,8},{8,0},{1,9},{9,1},{2,10},{10,2},{3,11},{11,3},{4,12},{12,4},... | collective-permute-start | bytes 6291464 | tf_op jit(solution)/shard_map/ppermute | solution.py:199
  31.0 0.3 convolution_bitcast_fusion.1
  31.4 0.1 collective-permute-start.14
  31.5 3.5 %collective-permute-done.14 = f32[256,64]{0,1:T(8,128)S(1)} collective-permute-done((f32[256,64]{0,1:T(8,128)S(1)}, f32[256,64]{0,1:T(8,128)S(1)}, u32[]{:S(2)}, u32[]{:S(2)}) %collective-permute-start.14) | collective-permute-done | bytes 65568 | tf_op jit(solution)/shard_map/ppermute | solution.py:145
  35.0 3.1 %collective-permute-start.15 = (f32[128,64]{0,1:T(8,128)S(1)}, f32[128,64]{0,1:T(8,128)S(1)}, u32[]{:S(2)}, u32[]{:S(2)}) collective-permute-start(f32[128,64]{0,1:T(8,128)S(1)} %constant_dynamic-slice_fusion.1), channel_id=1, source_target_pairs={{0,16},{16,0},{1,17},{17,1},{2,18},{18,2},{3,19},{19,3},{4,20},{20... | collective-permute-start | bytes 98312 | tf_op jit(solution)/shard_map/ppermute | solution.py:145
  38.1 1.9 %collective-permute-done.15 = f32[128,64]{0,1:T(8,128)S(1)} collective-permute-done((f32[128,64]{0,1:T(8,128)S(1)}, f32[128,64]{0,1:T(8,128)S(1)}, u32[]{:S(2)}, u32[]{:S(2)}) %collective-permute-start.15) | collective-permute-done | bytes 32800 | tf_op jit(solution)/shard_map/ppermute | solution.py:145
  40.0 0.1 constant_dynamic-slice_fusion
  40.1 0.2 collective-permute-start.16
  40.3 5.3 %collective-permute-done.16 = f32[64,64]{0,1:T(8,128)S(1)} collective-permute-done((f32[64,64]{0,1:T(8,128)S(1)}, f32[64,64]{0,1:T(8,128)S(1)}, u32[]{:S(2)}, u32[]{:S(2)}) %collective-permute-start.16) | collective-permute-done | bytes 16416 | tf_op jit(solution)/shard_map/ppermute | solution.py:145
  45.6 1.6 %collective-permute-start.17 = (f32[64,64]{0,1:T(8,128)S(1)}, f32[64,64]{0,1:T(8,128)S(1)}, u32[]{:S(2)}, u32[]{:S(2)}) collective-permute-start(f32[64,64]{0,1:T(8,128)S(1)} %dynamic-slice_add_fusion), channel_id=1, source_target_pairs={{0,32},{32,0},{64,96},{96,64},{128,160},{160,128},{192,224},{224,1... | collective-permute-start | bytes 49160 | tf_op jit(solution)/shard_map/ppermute | solution.py:147
  47.2 2.4 %collective-permute-done.17 = f32[64,64]{0,1:T(8,128)S(1)} collective-permute-done((f32[64,64]{0,1:T(8,128)S(1)}, f32[64,64]{0,1:T(8,128)S(1)}, u32[]{:S(2)}, u32[]{:S(2)}) %collective-permute-start.17) | collective-permute-done | bytes 16416 | tf_op jit(solution)/shard_map/ppermute | solution.py:147
  49.6 6.5 %collective-permute-start.18 = (f32[64,64]{0,1:T(8,128)S(1)}, f32[64,64]{0,1:T(8,128)S(1)}, u32[]{:S(2)}, u32[]{:S(2)}) collective-permute-start(f32[64,64]{0,1:T(8,128)S(1)} %add.249), channel_id=1, source_target_pairs={{0,64},{32,96},{64,0},{96,32},{128,192},{160,224},{192,128},{224,1... | collective-permute-start | bytes 49160 | tf_op jit(solution)/shard_map/ppermute | solution.py:147
  56.1 1.9 %collective-permute-done.18 = f32[64,64]{0,1:T(8,128)S(1)} collective-permute-done((f32[64,64]{0,1:T(8,128)S(1)}, f32[64,64]{0,1:T(8,128)S(1)}, u32[]{:S(2)}, u32[]{:S(2)}) %collective-permute-start.18) | collective-permute-done | bytes 16416 | tf_op jit(solution)/shard_map/ppermute | solution.py:147
  58.0 6.3 %collective-permute-start.19 = (f32[64,64]{0,1:T(8,128)S(1)}, f32[64,64]{0,1:T(8,128)S(1)}, u32[]{:S(2)}, u32[]{:S(2)}) collective-permute-start(f32[64,64]{0,1:T(8,128)S(1)} %add.250), channel_id=1, source_target_pairs={{0,128},{32,160},{64,192},{96,224},{128,0},{160,32},{192,64},{224,... | collective-permute-start | bytes 49160 | tf_op jit(solution)/shard_map/ppermute | solution.py:147
  64.3 2.2 %collective-permute-done.19 = f32[64,64]{0,1:T(8,128)S(1)} collective-permute-done((f32[64,64]{0,1:T(8,128)S(1)}, f32[64,64]{0,1:T(8,128)S(1)}, u32[]{:S(2)}, u32[]{:S(2)}) %collective-permute-start.19) | collective-permute-done | bytes 16416 | tf_op jit(solution)/shard_map/ppermute | solution.py:147
  66.6 5.4 %collective-permute-done.20 = f32[64,64]{0,1:T(8,128)S(1)} collective-permute-done((f32[64,64]{0,1:T(8,128)S(1)}, f32[64,64]{0,1:T(8,128)S(1)}, u32[]{:S(2)}, u32[]{:S(2)}) %collective-permute-start.20) | collective-permute-done | bytes 16416 | tf_op jit(solution)/shard_map/ppermute | solution.py:149
  72.0 0.1 maximum_select_fusion.2
  72.0 1.0 collective-permute-start.21
  73.1 3.0 %collective-permute-done.21 = f32[128,64]{0,1:T(8,128)S(1)} collective-permute-done((f32[128,64]{0,1:T(8,128)S(1)}, f32[128,64]{0,1:T(8,128)S(1)}, u32[]{:S(2)}, u32[]{:S(2)}) %collective-permute-start.21) | collective-permute-done | bytes 32800 | tf_op jit(solution)/shard_map/ppermute | solution.py:149
  76.1 0.1 collective-permute-start.22
  76.2 3.4 %copy-done.2 = bf16[256,128,128]{2,1,0:T(8,128)(2,1)S(1)} copy-done((bf16[256,128,128]{2,1,0:T(8,128)(2,1)S(1)}, bf16[256,128,128]{2,1,0:T(8,128)(2,1)}, u32[]{:S(2)}) %copy-start.2) | copy-done | bytes 8388632
  79.6 2.4 %shard_map.122 = f32[128,64,128]{2,1,0:T(8,128)S(1)} custom-call(s32[528]{0:T(1024)S(1)} %copy-done.4, s32[2]{0:T(128)S(1)} %copy-done.6, bf16[8,64,128]{2,1,0:T(8,128)(2,1)S(1)} %bitcast_bitcast_fusion.refs_2_, bf16[8,64,128]{2,1,0:T(8,128)(2,1)S(1)} %collective-permute-done.3.refs_3_, bf16[256,128,128]{2,1,0:T(8,128)(2,1)S(1)} %copy-done.2), custom_call_target="tpu_custom_call" | custom-call | flops 268435456 | bytes 8388608 | tf_op jit(solution)/shard_map/pallas_call | solution.py:93
  82.0 0.7 fusion.61
  82.6 2.8 %fusion.55 = (bf16[128,64,128]{2,1,0:T(8,128)(2,1)S(1)}, f32[128,64,128]{2,1,0:T(8,128)S(1)}) fusion(f32[128,64,128]{2,1,0:T(8,128)S(1)} %shard_map.122, bf16[128,64,128]{2,1,0:T(8,128)(2,1)} %collective-permute-done.4), kind=kLoop, calls=%fused_computation.146 | loop fusion | flops 3145728 | bytes 12582912 | tf_op jit(solution)/shard_map/convert.5
  85.4 1.1 collective-permute-start.5
  86.6 15.1 %collective-permute-start.6 = (bf16[2,4,2,64,128]{4,3,2,1,0:T(8,128)(2,1)S(1)}, bf16[2,4,2,64,128]{4,3,2,1,0:T(8,128)(2,1)S(1)}, u32[]{:S(2)}, u32[]{:S(2)}) collective-permute-start(bf16[2,4,2,64,128]{4,3,2,1,0:T(8,128)(2,1)S(1)} %bitcast.78), channel_id=1, source_target_pairs={{0,224},{32,64},{64,32},{96,128},{128,96},{160,192},{192,160},{224... | collective-permute-start | bytes 786440 | tf_op jit(solution)/shard_map/ppermute | solution.py:120
  101.7 0.1 fusion.59
  101.8 0.1 fusion.58
  102.0 0.1 collective-permute-start.8
  102.1 4.0 %collective-permute-done.6 = bf16[2,4,2,64,128]{4,3,2,1,0:T(8,128)(2,1)S(1)} collective-permute-done((bf16[2,4,2,64,128]{4,3,2,1,0:T(8,128)(2,1)S(1)}, bf16[2,4,2,64,128]{4,3,2,1,0:T(8,128)(2,1)S(1)}, u32[]{:S(2)}, u32[]{:S(2)}) %collective-permute-start.6) | collective-permute-done | bytes 262176 | tf_op jit(solution)/shard_map/ppermute | solution.py:120
  106.3 0.1 collective-permute-start.7
  106.4 10.0 %collective-permute-done.8 = bf16[2,4,4,64,128]{4,3,2,1,0:T(8,128)(2,1)S(1)} collective-permute-done((bf16[2,4,4,64,128]{4,3,2,1,0:T(8,128)(2,1)S(1)}, bf16[2,4,4,64,128]{4,3,2,1,0:T(8,128)(2,1)S(1)}, u32[]{:S(2)}, u32[]{:S(2)}) %collective-permute-start.8) | collective-permute-done | bytes 524320 | tf_op jit(solution)/shard_map/ppermute | solution.py:122
  116.4 0.2 fusion.56
  116.7 0.1 collective-permute-start.9
  116.8 0.6 collective-permute-start.10
  117.4 1.8 %collective-permute-done.7 = bf16[4,4,64,128]{3,2,1,0:T(8,128)(2,1)S(1)} collective-permute-done((bf16[4,4,64,128]{3,2,1,0:T(8,128)(2,1)S(1)}, bf16[4,4,64,128]{3,2,1,0:T(8,128)(2,1)S(1)}, u32[]{:S(2)}, u32[]{:S(2)}) %collective-permute-start.7) | collective-permute-done | bytes 262176 | tf_op jit(solution)/shard_map/ppermute | solution.py:125
  119.3 2.4 %collective-permute-done.9 = bf16[4,2,64,128]{3,2,1,0:T(8,128)(2,1)S(1)} collective-permute-done((bf16[4,2,64,128]{3,2,1,0:T(8,128)(2,1)S(1)}, bf16[4,2,64,128]{3,2,1,0:T(8,128)(2,1)S(1)}, u32[]{:S(2)}, u32[]{:S(2)}) %collective-permute-start.9) | collective-permute-done | bytes 131104 | tf_op jit(solution)/shard_map/ppermute | solution.py:126
  121.7 3.5 %collective-permute-done.10 = bf16[4,2,64,128]{3,2,1,0:T(8,128)(2,1)S(1)} collective-permute-done((bf16[4,2,64,128]{3,2,1,0:T(8,128)(2,1)S(1)}, bf16[4,2,64,128]{3,2,1,0:T(8,128)(2,1)S(1)}, u32[]{:S(2)}, u32[]{:S(2)}) %collective-permute-start.10) | collective-permute-done | bytes 131104 | tf_op jit(solution)/shard_map/ppermute | solution.py:127
  125.3 0.1 fusion.54
  125.4 0.1 collective-permute-start.11
  125.5 5.9 %collective-permute-start.13 = (bf16[8,64,128]{2,1,0:T(8,128)(2,1)S(1)}, bf16[8,64,128]{2,1,0:T(8,128)(2,1)S(1)}, u32[]{:S(2)}, u32[]{:S(2)}) collective-permute-start(bf16[8,64,128]{2,1,0:T(8,128)(2,1)S(1)} %get-tuple-element.20), channel_id=1, source_target_pairs={{0,128},{32,160},{64,192},{96,224},{128,0},{160,32},{192,64},{224,... | collective-permute-start | bytes 393224 | tf_op jit(solution)/shard_map/ppermute | solution.py:134
  131.4 4.0 %collective-permute-start.12 = (bf16[8,64,128]{2,1,0:T(8,128)(2,1)S(1)}, bf16[8,64,128]{2,1,0:T(8,128)(2,1)S(1)}, u32[]{:S(2)}, u32[]{:S(2)}) collective-permute-start(bf16[8,64,128]{2,1,0:T(8,128)(2,1)S(1)} %get-tuple-element.21), channel_id=1, source_target_pairs={{0,192},{32,224},{64,0},{96,32},{128,64},{160,96},{192,128},{224,1... | collective-permute-start | bytes 393224 | tf_op jit(solution)/shard_map/ppermute | solution.py:134
  135.4 0.1 pad_maximum_fusion.1
  135.6 0.1 collective-permute-done.13
  135.7 2.3 %collective-permute-done.12 = bf16[8,64,128]{2,1,0:T(8,128)(2,1)S(1)} collective-permute-done((bf16[8,64,128]{2,1,0:T(8,128)(2,1)S(1)}, bf16[8,64,128]{2,1,0:T(8,128)(2,1)S(1)}, u32[]{:S(2)}, u32[]{:S(2)}) %collective-permute-start.12) | collective-permute-done | bytes 131104 | tf_op jit(solution)/shard_map/ppermute | solution.py:134
  138.0 0.7 fusion.18
  (42 shorter events, 0.6 us)
Async XLA Ops:
  0.6 13.9 %copy-start = (bf16[256,1024]{1,0:T(8,128)(2,1)S(1)}, bf16[256,1024]{1,0:T(8,128)(2,1)}, u32[]{:S(2)}) copy-start(bf16[256,1024]{1,0:T(8,128)(2,1)} %param.13) | copy-start | bytes 1572868
  1.7 8.9 %collective-permute-start.2 = (bf16[64,1024]{1,0:T(8,128)(2,1)S(1)}, bf16[64,1024]{1,0:T(8,128)(2,1)S(1)}, u32[]{:S(2)}, u32[]{:S(2)}) collective-permute-start(bf16[64,1024]{1,0:T(8,128)(2,1)S(1)} %compare_select_fusion), channel_id=1, source_target_pairs={{0,3},{1,0},{2,1},{3,2},{4,7},{5,4},{6,5},{7,6},{8,11},{9,8},{10,9... | collective-permute-start | bytes 393224 | tf_op jit(solution)/shard_map/ppermute | solution.py:170
  4.5 7.9 %collective-permute-start.1 = (bf16[64,1024]{1,0:T(8,128)(2,1)S(1)}, bf16[64,1024]{1,0:T(8,128)(2,1)S(1)}, u32[]{:S(2)}, u32[]{:S(2)}) collective-permute-start(bf16[64,1024]{1,0:T(8,128)(2,1)S(1)} %compare_select_fusion), channel_id=1, source_target_pairs={{0,2},{1,3},{2,0},{3,1},{4,6},{5,7},{6,4},{7,5},{8,10},{9,11},{10,... | collective-permute-start | bytes 393224 | tf_op jit(solution)/shard_map/ppermute | solution.py:170
  5.3 8.5 %collective-permute-start = (bf16[64,1024]{1,0:T(8,128)(2,1)S(1)}, bf16[64,1024]{1,0:T(8,128)(2,1)S(1)}, u32[]{:S(2)}, u32[]{:S(2)}) collective-permute-start(bf16[64,1024]{1,0:T(8,128)(2,1)S(1)} %compare_select_fusion), channel_id=1, source_target_pairs={{0,1},{1,2},{2,3},{3,0},{4,5},{5,6},{6,7},{7,4},{8,9},{9,10},{10,1... | collective-permute-start | bytes 393224 | tf_op jit(solution)/shard_map/ppermute | solution.py:170
  14.1 6.9 %copy-start.8 = (f32[128,1024]{1,0:T(8,128)}, f32[128,1024]{1,0:T(8,128)S(1)}, u32[]{:S(2)}) copy-start(f32[128,1024]{1,0:T(8,128)S(1)} %fusion.9) | copy-start | bytes 1572868
  14.1 6.8 %collective-permute-start.3 = (bf16[8,64,128]{2,1,0:T(8,128)(2,1)S(1)}, bf16[8,64,128]{2,1,0:T(8,128)(2,1)S(1)}, u32[]{:S(2)}, u32[]{:S(2)}) collective-permute-start(bf16[8,64,128]{2,1,0:T(8,128)(2,1)S(1)} %bitcast_bitcast_fusion.refs_2_), channel_id=1, source_target_pairs={{0,4},{4,0},{1,5},{5,1},{2,6},{6,2},{3,7},{7,3},{8,12},{12,8},{9,1... | collective-permute-start | bytes 393224 | tf_op jit(solution)/shard_map/ppermute | solution.py:179
  20.9 3.4 %copy-start.1 = (bf16[256,128,128]{2,1,0:T(8,128)(2,1)S(1)}, bf16[256,128,128]{2,1,0:T(8,128)(2,1)}, u32[]{:S(2)}) copy-start(bf16[256,128,128]{2,1,0:T(8,128)(2,1)} %refs_4_.3) | copy-start | bytes 25165828
  24.3 0.7 copy-start.3
  25.0 0.6 copy-start.5
  25.6 5.4 %copy-start.7 = (bf16[256,1024]{1,0:T(8,128)(2,1)S(1)}, bf16[256,1024]{1,0:T(8,128)(2,1)}, u32[]{:S(2)}) copy-start(bf16[256,1024]{1,0:T(8,128)(2,1)} %param.12) | copy-start | bytes 1572868
  25.6 50.5 %copy-start.4 = (s32[528]{0:T(1024)S(1)}, s32[528]{0:T(1024)}, u32[]{:S(2)}) copy-start(s32[528]{0:T(1024)} %get-tuple-element.5.refs_0_) | copy-start | bytes 6340
  25.6 50.6 %copy-start.6 = (s32[2]{0:T(128)S(1)}, s32[2]{0:T(128)}, u32[]{:S(2)}) copy-start(s32[2]{0:T(128)} %get-tuple-element.6.refs_1_) | copy-start | bytes 28
  28.5 54.1 %collective-permute-start.4 = (bf16[128,64,128]{2,1,0:T(8,128)(2,1)S(1)}, bf16[128,64,128]{2,1,0:T(8,128)(2,1)}, u32[]{:S(2)}, u32[]{:S(2)}) collective-permute-start(bf16[128,64,128]{2,1,0:T(8,128)(2,1)S(1)} %shard_map.123), channel_id=1, source_target_pairs={{0,8},{8,0},{1,9},{9,1},{2,10},{10,2},{3,11},{11,3},{4,12},{12,4},... | collective-permute-start | bytes 6291464 | tf_op jit(solution)/shard_map/ppermute | solution.py:199
  31.4 3.6 %collective-permute-start.14 = (f32[256,64]{0,1:T(8,128)S(1)}, f32[256,64]{0,1:T(8,128)S(1)}, u32[]{:S(2)}, u32[]{:S(2)}) collective-permute-start(f32[256,64]{0,1:T(8,128)S(1)} %fusion.26), channel_id=1, source_target_pairs={{0,8},{8,0},{1,9},{9,1},{2,10},{10,2},{3,11},{11,3},{4,12},{12,4},... | collective-permute-start | bytes 196616 | tf_op jit(solution)/shard_map/ppermute | solution.py:145
  35.0 5.1 %collective-permute-start.15 = (f32[128,64]{0,1:T(8,128)S(1)}, f32[128,64]{0,1:T(8,128)S(1)}, u32[]{:S(2)}, u32[]{:S(2)}) collective-permute-start(f32[128,64]{0,1:T(8,128)S(1)} %constant_dynamic-slice_fusion.1), channel_id=1, source_target_pairs={{0,16},{16,0},{1,17},{17,1},{2,18},{18,2},{3,19},{19,3},{4,20},{20... | collective-permute-start | bytes 98312 | tf_op jit(solution)/shard_map/ppermute | solution.py:145
  40.1 5.4 %collective-permute-start.16 = (f32[64,64]{0,1:T(8,128)S(1)}, f32[64,64]{0,1:T(8,128)S(1)}, u32[]{:S(2)}, u32[]{:S(2)}) collective-permute-start(f32[64,64]{0,1:T(8,128)S(1)} %constant_dynamic-slice_fusion), channel_id=1, source_target_pairs={{0,4},{4,0},{1,5},{5,1},{2,6},{6,2},{3,7},{7,3},{8,12},{12,8},{9,1... | collective-permute-start | bytes 49160 | tf_op jit(solution)/shard_map/ppermute | solution.py:145
  45.6 3.9 %collective-permute-start.17 = (f32[64,64]{0,1:T(8,128)S(1)}, f32[64,64]{0,1:T(8,128)S(1)}, u32[]{:S(2)}, u32[]{:S(2)}) collective-permute-start(f32[64,64]{0,1:T(8,128)S(1)} %dynamic-slice_add_fusion), channel_id=1, source_target_pairs={{0,32},{32,0},{64,96},{96,64},{128,160},{160,128},{192,224},{224,1... | collective-permute-start | bytes 49160 | tf_op jit(solution)/shard_map/ppermute | solution.py:147
  49.6 8.4 %collective-permute-start.18 = (f32[64,64]{0,1:T(8,128)S(1)}, f32[64,64]{0,1:T(8,128)S(1)}, u32[]{:S(2)}, u32[]{:S(2)}) collective-permute-start(f32[64,64]{0,1:T(8,128)S(1)} %add.249), channel_id=1, source_target_pairs={{0,64},{32,96},{64,0},{96,32},{128,192},{160,224},{192,128},{224,1... | collective-permute-start | bytes 49160 | tf_op jit(solution)/shard_map/ppermute | solution.py:147
  58.0 8.6 %collective-permute-start.19 = (f32[64,64]{0,1:T(8,128)S(1)}, f32[64,64]{0,1:T(8,128)S(1)}, u32[]{:S(2)}, u32[]{:S(2)}) collective-permute-start(f32[64,64]{0,1:T(8,128)S(1)} %add.250), channel_id=1, source_target_pairs={{0,128},{32,160},{64,192},{96,224},{128,0},{160,32},{192,64},{224,... | collective-permute-start | bytes 49160 | tf_op jit(solution)/shard_map/ppermute | solution.py:147
  66.5 5.4 %collective-permute-start.20 = (f32[64,64]{0,1:T(8,128)S(1)}, f32[64,64]{0,1:T(8,128)S(1)}, u32[]{:S(2)}, u32[]{:S(2)}) collective-permute-start(f32[64,64]{0,1:T(8,128)S(1)} %add.251), channel_id=1, source_target_pairs={{0,4},{4,0},{1,5},{5,1},{2,6},{6,2},{3,7},{7,3},{8,12},{12,8},{9,1... | collective-permute-start | bytes 49160 | tf_op jit(solution)/shard_map/ppermute | solution.py:149
  72.0 4.0 %collective-permute-start.21 = (f32[128,64]{0,1:T(8,128)S(1)}, f32[128,64]{0,1:T(8,128)S(1)}, u32[]{:S(2)}, u32[]{:S(2)}) collective-permute-start(f32[128,64]{0,1:T(8,128)S(1)} %maximum_select_fusion.2), channel_id=1, source_target_pairs={{0,16},{16,0},{1,17},{17,1},{2,18},{18,2},{3,19},{19,3},{4,20},{20... | collective-permute-start | bytes 98312 | tf_op jit(solution)/shard_map/ppermute | solution.py:149
  76.1 5.9 %collective-permute-start.22 = (f32[256,64]{0,1:T(8,128)S(1)}, f32[256,64]{0,1:T(8,128)S(1)}, u32[]{:S(2)}, u32[]{:S(2)}) collective-permute-start(f32[256,64]{0,1:T(8,128)S(1)} %maximum_select_fusion.1), channel_id=1, source_target_pairs={{0,8},{8,0},{1,9},{9,1},{2,10},{10,2},{3,11},{11,3},{4,12},{12,4},... | collective-permute-start | bytes 196616 | tf_op jit(solution)/shard_map/ppermute | solution.py:149
  76.2 3.4 %copy-start.2 = (bf16[256,128,128]{2,1,0:T(8,128)(2,1)S(1)}, bf16[256,128,128]{2,1,0:T(8,128)(2,1)}, u32[]{:S(2)}) copy-start(bf16[256,128,128]{2,1,0:T(8,128)(2,1)} %refs_4_.3) | copy-start | bytes 25165828
  85.4 20.7 %collective-permute-start.5 = (bf16[2,4,2,64,128]{4,3,2,1,0:T(8,128)(2,1)S(1)}, bf16[2,4,2,64,128]{4,3,2,1,0:T(8,128)(2,1)S(1)}, u32[]{:S(2)}, u32[]{:S(2)}) collective-permute-start(bf16[2,4,2,64,128]{4,3,2,1,0:T(8,128)(2,1)S(1)} %bitcast.77), channel_id=1, source_target_pairs={{0,32},{32,0},{64,96},{96,64},{128,160},{160,128},{192,224},{224,1... | collective-permute-start | bytes 786440 | tf_op jit(solution)/shard_map/ppermute | solution.py:119
  86.6 19.5 %collective-permute-start.6 = (bf16[2,4,2,64,128]{4,3,2,1,0:T(8,128)(2,1)S(1)}, bf16[2,4,2,64,128]{4,3,2,1,0:T(8,128)(2,1)S(1)}, u32[]{:S(2)}, u32[]{:S(2)}) collective-permute-start(bf16[2,4,2,64,128]{4,3,2,1,0:T(8,128)(2,1)S(1)} %bitcast.78), channel_id=1, source_target_pairs={{0,224},{32,64},{64,32},{96,128},{128,96},{160,192},{192,160},{224... | collective-permute-start | bytes 786440 | tf_op jit(solution)/shard_map/ppermute | solution.py:120
  102.0 14.4 %collective-permute-start.8 = (bf16[2,4,4,64,128]{4,3,2,1,0:T(8,128)(2,1)S(1)}, bf16[2,4,4,64,128]{4,3,2,1,0:T(8,128)(2,1)S(1)}, u32[]{:S(2)}, u32[]{:S(2)}) collective-permute-start(bf16[2,4,4,64,128]{4,3,2,1,0:T(8,128)(2,1)S(1)} %fusion.7), channel_id=1, source_target_pairs={{0,16},{16,0},{1,17},{17,1},{2,18},{18,2},{3,19},{19,3},{4,20},{20... | collective-permute-start | bytes 1572872 | tf_op jit(solution)/shard_map/ppermute | solution.py:122
  106.3 12.9 %collective-permute-start.7 = (bf16[4,4,64,128]{3,2,1,0:T(8,128)(2,1)S(1)}, bf16[4,4,64,128]{3,2,1,0:T(8,128)(2,1)S(1)}, u32[]{:S(2)}, u32[]{:S(2)}) collective-permute-start(bf16[4,4,64,128]{3,2,1,0:T(8,128)(2,1)S(1)} %fusion.17), channel_id=1, source_target_pairs={{0,16},{16,0},{1,17},{17,1},{2,18},{18,2},{3,19},{19,3},{4,20},{20... | collective-permute-start | bytes 786440 | tf_op jit(solution)/shard_map/ppermute | solution.py:125
  116.6 21.3 %copy-start.9 = (f32[128,1024]{1,0:T(8,128)S(1)}, f32[128,1024]{1,0:T(8,128)}, u32[]{:S(2)}) copy-start(f32[128,1024]{1,0:T(8,128)} %copy-done.8) | copy-start | bytes 1572868
  116.7 5.1 %collective-permute-start.9 = (bf16[4,2,64,128]{3,2,1,0:T(8,128)(2,1)S(1)}, bf16[4,2,64,128]{3,2,1,0:T(8,128)(2,1)S(1)}, u32[]{:S(2)}, u32[]{:S(2)}) collective-permute-start(bf16[4,2,64,128]{3,2,1,0:T(8,128)(2,1)S(1)} %get-tuple-element.22), channel_id=1, source_target_pairs={{0,32},{32,0},{64,96},{96,64},{128,160},{160,128},{192,224},{224,1... | collective-permute-start | bytes 393224 | tf_op jit(solution)/shard_map/ppermute | solution.py:126
  116.8 8.4 %collective-permute-start.10 = (bf16[4,2,64,128]{3,2,1,0:T(8,128)(2,1)S(1)}, bf16[4,2,64,128]{3,2,1,0:T(8,128)(2,1)S(1)}, u32[]{:S(2)}, u32[]{:S(2)}) collective-permute-start(bf16[4,2,64,128]{3,2,1,0:T(8,128)(2,1)S(1)} %get-tuple-element.23), channel_id=1, source_target_pairs={{0,224},{32,64},{64,32},{96,128},{128,96},{160,192},{192,160},{224... | collective-permute-start | bytes 393224 | tf_op jit(solution)/shard_map/ppermute | solution.py:127
  125.4 10.2 %collective-permute-start.11 = (bf16[8,64,128]{2,1,0:T(8,128)(2,1)S(1)}, bf16[8,64,128]{2,1,0:T(8,128)(2,1)S(1)}, u32[]{:S(2)}, u32[]{:S(2)}) collective-permute-start(bf16[8,64,128]{2,1,0:T(8,128)(2,1)S(1)} %get-tuple-element.19), channel_id=1, source_target_pairs={{0,64},{32,96},{64,128},{96,160},{128,192},{160,224},{192,0},{224,... | collective-permute-start | bytes 393224 | tf_op jit(solution)/shard_map/ppermute | solution.py:134
  125.5 10.2 %collective-permute-start.13 = (bf16[8,64,128]{2,1,0:T(8,128)(2,1)S(1)}, bf16[8,64,128]{2,1,0:T(8,128)(2,1)S(1)}, u32[]{:S(2)}, u32[]{:S(2)}) collective-permute-start(bf16[8,64,128]{2,1,0:T(8,128)(2,1)S(1)} %get-tuple-element.20), channel_id=1, source_target_pairs={{0,128},{32,160},{64,192},{96,224},{128,0},{160,32},{192,64},{224,... | collective-permute-start | bytes 393224 | tf_op jit(solution)/shard_map/ppermute | solution.py:134
  131.4 6.6 %collective-permute-start.12 = (bf16[8,64,128]{2,1,0:T(8,128)(2,1)S(1)}, bf16[8,64,128]{2,1,0:T(8,128)(2,1)S(1)}, u32[]{:S(2)}, u32[]{:S(2)}) collective-permute-start(bf16[8,64,128]{2,1,0:T(8,128)(2,1)S(1)} %get-tuple-element.21), channel_id=1, source_target_pairs={{0,192},{32,224},{64,0},{96,32},{128,64},{160,96},{192,128},{224,1... | collective-permute-start | bytes 393224 | tf_op jit(solution)/shard_map/ppermute | solution.py:134

commit v2 on v1

v2 whole, which is shorter than its diff:
```python
import jax
import jax.numpy as jnp
from jax import lax
from jax.experimental import pallas as pl
from jax.experimental.pallas import tpu as pltpu
from jax.sharding import Mesh, PartitionSpec as P

AXES = ("z", "pair", "core", "half", "x")
BLOCK = 128
GROUP = 8
BIG = 32
LISTS = 2
PLACES = 128
ROOM = 256 + LISTS * GROUP
SCOPED = 16 * 1024 * 1024


def swap(n):
    return [(i, i ^ 1) for i in range(n)]


def turn(k, n):
    return [(i, (i + k) % n) for i in range(n)]


EVEN_PAIRS = swap(8)
ODD_PAIRS = [(i, (((i + 1) % 8 ^ 1) - 1) % 8) for i in range(8)]


def list_kernel(table_ref, vals_ref, lists_ref, starts_ref, tiles_ref, sem):
    slots = vals_ref.shape[0]
    steps = (table_ref[2 * slots + LISTS + 1] + GROUP - 1) // GROUP
    starts_ref[0] = table_ref[2 * slots]
    for i in range(1, LISTS + 1):
        end = table_ref[2 * slots + i]
        starts_ref[i] = end
        for k in range(GROUP - 1):
            lists_ref[jnp.maximum(end - 1 - k, 0)] = jnp.int32(PLACES)

    def place(step, carry):
        for k in range(GROUP):
            slot = step * GROUP + k
            spot = table_ref[slot]
            lists_ref[spot] = table_ref[slots + slot]
            pltpu.make_async_copy(vals_ref.at[slot], tiles_ref.at[spot], sem).start()
        return carry

    def finish(step, carry):
        some = pl.ds(0, GROUP)
        pltpu.make_async_copy(vals_ref.at[some], tiles_ref.at[some], sem).wait()
        return carry

    lax.fori_loop(0, steps, place, 0)
    lax.fori_loop(0, steps, finish, 0)


def make_lists(live, entries, which, vals):
    slots = jnp.arange(vals.shape[0], dtype=jnp.int32)
    which = jnp.where(slots < live, which, LISTS)
    earlier = (which[:, None] == which[None, :]) & (slots[:, None] > slots[None, :])
    rank = jnp.sum(earlier.astype(jnp.int32), axis=1)
    starts = [jnp.int32(0)]
    for i in range(LISTS):
        held = jnp.sum((which == i).astype(jnp.int32))
        starts.append(starts[-1] + (held + GROUP - 1) // GROUP * GROUP)
    spots = ROOM + slots % GROUP
    for i in range(LISTS):
        spots = jnp.where(which == i, starts[i] + rank, spots)
    table = jnp.concatenate([spots, entries, jnp.stack(starts + [live])])
    smem = pl.BlockSpec(memory_space=pltpu.SMEM)
    return pl.pallas_call(
        list_kernel,
        out_shape=(
            pltpu.SMEM((ROOM + GROUP,), jnp.int32),
            pltpu.SMEM((LISTS + 1,), jnp.int32),
            pltpu.VMEM((ROOM + GROUP, BLOCK, BLOCK), vals.dtype),
        ),
        in_specs=[smem, pl.BlockSpec(memory_space=pl.ANY)],
        out_specs=(smem, smem, pl.BlockSpec(memory_space=pltpu.VMEM)),
        scratch_shapes=[pltpu.SemaphoreType.DMA],
        compiler_params=pltpu.CompilerParams(vmem_limit_bytes=SCOPED),
        cost_estimate=pl.CostEstimate(flops=0, bytes_accessed=12 << 20, transcendentals=0),
    )(table, pltpu.with_memory_space_constraint(vals, pltpu.HBM))


def tile_kernel(which, lists_ref, starts_ref, near_ref, far_ref, tiles_ref, first_ref, last_ref, total, panel):
    start, end = starts_ref[which], starts_ref[which + 1]
    panel[0:8] = near_ref[...]
    panel[8:16] = far_ref[...]
    total[...] = jnp.zeros_like(total)

    def add(base, count):
        entries = [lists_ref[base + k] for k in range(count)]
        products = [
            jnp.dot(panel[entry // 256], tiles_ref[base + k], preferred_element_type=jnp.float32)
            for k, entry in enumerate(entries)
        ]
        for entry, product in zip(entries, products):
            total[entry & 255] += product

    def big(step, carry):
        add(start + step * BIG, BIG)
        return carry

    def small(step, carry):
        add(start + step * GROUP, GROUP)
        return carry

    bigs = (end - start) // BIG
    lax.fori_loop(0, bigs, big, 0)
    lax.fori_loop(bigs * (BIG // GROUP), (end - start) // GROUP, small, 0)
    n = PLACES // 2
    first_ref[...] = total[0:n].astype(first_ref.dtype)
    last_ref[...] = total[n : 2 * n].astype(last_ref.dtype)


def tile_sums(which, lists, starts, near, far, tiles, dtype):
    rows = near.shape[1]
    smem = pl.BlockSpec(memory_space=pltpu.SMEM)
    vmem = pl.BlockSpec(memory_space=pltpu.VMEM)
    return pl.pallas_call(
        lambda *refs: tile_kernel(which, *refs),
        out_shape=(jax.ShapeDtypeStruct((PLACES // 2, rows, BLOCK), dtype),) * 2,
        in_specs=[smem, smem, vmem, vmem, vmem],
        out_specs=(vmem, vmem),
        scratch_shapes=[
            pltpu.VMEM((PLACES + 1, rows, BLOCK), jnp.float32),
            pltpu.VMEM((16, rows, BLOCK), jnp.bfloat16),
        ],
        compiler_params=pltpu.CompilerParams(vmem_limit_bytes=SCOPED),
        cost_estimate=pl.CostEstimate(flops=2 * 64 * rows * 128 * 128, bytes_accessed=4 << 20, transcendentals=0),
    )(
        pltpu.with_memory_space_constraint(lists, pltpu.SMEM),
        pltpu.with_memory_space_constraint(starts, pltpu.SMEM),
        near,
        far,
        pltpu.with_memory_space_constraint(tiles, pltpu.VMEM),
    )


def half16(x):
    return x.astype(jnp.bfloat16)


def wide(x):
    return x.astype(jnp.float32)


def under(core_sum, shape):
    return core_sum.reshape(*shape, *core_sum.shape[1:])


def weight_steps():
    def give(axis):
        me = lax.axis_index(axis)

        def step(part):
            n = part.shape[0] // 2
            mine = lax.dynamic_slice_in_dim(part, me * n, n, 0)
            other = lax.dynamic_slice_in_dim(part, (1 - me) * n, n, 0)
            return mine + lax.ppermute(other, axis, swap(2))

        return step

    def join(axis, k):
        return lambda part: part + lax.ppermute(part, axis, [(i, i ^ k) for i in range(lax.axis_size(axis))])

    def collect(axis):
        me = lax.axis_index(axis)

        def step(part):
            came = lax.ppermute(part, axis, swap(2))
            return jnp.where(me == 0, jnp.concatenate([part, came]), jnp.concatenate([came, part]))

        return step

    return iter(
        [give("core"), join("z", 1), join("z", 2), join("z", 4), join("pair", 1), join("half", 1), collect("core")]
    )


def beside(steps, count, part, *others):
    for _ in range(count):
        part = next(steps)(part)
    return lax.optimization_barrier((part, *others))


def contract_nodes(left, right):
    return lax.dot_general(left, right, (((1,), (1,)), ((), ())), preferred_element_type=jnp.float32)


def on_device(
    cotangent, preact, features, aggregated, w_self, w_neigh, tile_rows, tile_cols, tile_vals, tile_live
):
    z, pair, core, half, x = (lax.axis_index(a) for a in AXES)
    delta = jnp.where(preact > 0, cotangent, jnp.zeros_like(cotangent))
    rows, nodes = delta.shape
    in_width = w_self.shape[0]

    steps = weight_steps()
    part = jnp.concatenate([contract_nodes(features, delta), contract_nodes(aggregated, delta)], axis=0)
    hidden = [lax.ppermute(delta, "x", turn(k, 4)) for k in (1, 2, 3)]
    part, *hidden = beside(steps, 1, part, *hidden)
    hidden = [delta] + hidden
    weights = jnp.concatenate(
        [lax.dynamic_slice_in_dim(w, x * rows, rows, 0) for w in (w_neigh, w_self)], axis=0
    )
    weights = jnp.concatenate(
        [lax.dynamic_slice_in_dim(weights, (x + 4 - k) % 4 * rows, rows, 1) for k in range(4)], axis=1
    )
    both = jnp.dot(weights, jnp.concatenate(hidden, axis=0), preferred_element_type=jnp.float32)
    near = half16(both[:rows]).reshape(rows, nodes // BLOCK, BLOCK).transpose(1, 0, 2)
    part, near = lax.optimization_barrier((part, near))
    far = lax.ppermute(near, "half", swap(2))
    part, far = beside(steps, 1, part, far)
    self_term = both[rows:]

    owner, within = tile_cols // 16, tile_cols % 8
    late, odd = within // 4, within // 2 % 2
    at, me = (owner // 4 + odd) % 8, (z + odd) % 8
    step = (at % 2) ^ (me % 2)
    turns = (at // 2 - me // 2 + 4) % 4
    across = (owner // 2 % 2) ^ pair
    place = jnp.where(late == 1, (across * 2 + odd) * 2 + step, (step * 2 + odd) * 2 + across)
    place = ((1 - late) * 8 + place) * 8 + turns * 2 + within % 2
    block = (tile_rows - (z * 4 + pair * 2 + core) * 16) ^ (half * 8)
    which = 1 - ((owner % 2) ^ core).astype(jnp.int32)
    lists, starts, tiles = make_lists(tile_live[0], block * 256 + place, which, tile_vals)

    away_late, away_early = tile_sums(0, lists, starts, near, far, tiles, jnp.bfloat16)
    came_late = lax.ppermute(away_late, "core", swap(2))
    came_early = lax.ppermute(away_early, "core", swap(2))
    late, early = tile_sums(1, lists, starts, near, far, tiles, jnp.float32)
    late = under(late + wide(came_late), (2, 2, 2, 4, 2))
    came_late = lax.ppermute(half16(late[1]), "pair", swap(2))
    early = under(early + wide(came_early), (2, 2, 2, 4, 2))
    even, odd_ones = half16(early[1, 0]), half16(early[1, 1])
    part, even, odd_ones = beside(steps, 1, part, even, odd_ones)
    came_even = lax.ppermute(even, "z", EVEN_PAIRS)
    came_odd = lax.ppermute(odd_ones, "z", ODD_PAIRS)
    part, came_even, came_odd, came_late = beside(steps, 1, part, came_even, came_odd, came_late)

    early = early[0] + wide(jnp.stack([came_even, came_odd]))
    late = late[0] + wide(came_late)
    across, even, odd_ones = half16(early[:, 1]), half16(late[0, 1]), half16(late[1, 1])
    part, across, even, odd_ones = lax.optimization_barrier((part, across, even, odd_ones))
    came_early = lax.ppermute(across, "pair", swap(2))
    came_even = lax.ppermute(even, "z", EVEN_PAIRS)
    came_odd = lax.ppermute(odd_ones, "z", ODD_PAIRS)
    part, came_early, came_even, came_odd = beside(steps, 1, part, came_early, came_even, came_odd)

    early = early[:, 0] + wide(came_early)
    late = late[:, 0] + wide(jnp.stack([came_even, came_odd]))
    both = jnp.concatenate([early, late], axis=0)
    rounded = half16(both)
    came = [lax.ppermute(rounded[:, k], "z", turn(2 * k, 8)) for k in (1, 3, 2)]
    part, came[0] = lax.optimization_barrier((part, came[0]))
    for step in steps:
        part = step(part)
    summed = both[:, 0] + wide(came[0]) + wide(came[1]) + wide(came[2])
    summed = summed.reshape(8, rows, BLOCK).transpose(1, 0, 2).reshape(rows, nodes)
    input_grad = half16(summed + self_term)
    return (input_grad, part[:in_width], part[in_width:])


def solution(mesh):
    nodes = ("z", "pair", "core", "half")
    return jax.shard_map(
        on_device,
        mesh=Mesh(mesh.devices.reshape(8, 2, 2, 2, 4), AXES),
        in_specs=(
            P("x", nodes),
            P("x", nodes),
            P(None, nodes),
            P(None, nodes),
            P(),
            P(),
            P(nodes),
            P(nodes),
            P(nodes, None, None),
            P(nodes),
        ),
        out_specs=(P("x", nodes), P(None, "x"), P(None, "x")),
        check_vma=False,
    )
```

time: 140 us -> 80.3 us (0.57)
  the two profiles are of different devices: /device:TPU:16 before, /device:TPU:1 now
where the time goes in v2:
time: 80.3 us; the launch traced here: 79.6 us
  starting transfers between devices  36.3 us (45%)
  waiting for transfers between devices  24.7 us (31%)
  Pallas kernels  7.4 us (9%)
  other arithmetic  4.2 us (5%)
  between operations  3.05 us (4%)
  local copies, waits for them, and re-layouts  2.01 us (3%)
  matrix products  1.88 us (2%)
    ppermute x5, waiting for transfers between devices, join(): lax.ppermute(part, axis, [(i, i ^ k) for i in range(lax.axis_size(axis))])  11.6 us
    ppermute x3, waiting for transfers between devices, on_device(): came = [lax.ppermute(rounded[:, k], 'z', turn(2 * k, 8)) for k in (1, 3, 2)]  10.7 us
    ppermute x5, starting transfers between devices, join(): lax.ppermute(part, axis, [(i, i ^ k) for i in range(lax.axis_size(axis))])  7.86 us
    ppermute x3, starting transfers between devices, on_device(): came = [lax.ppermute(rounded[:, k], 'z', turn(2 * k, 8)) for k in (1, 3, 2)]  7.54 us
    ppermute x3, starting transfers between devices, on_device(): hidden = [lax.ppermute(delta, 'x', turn(k, 4)) for k in (1, 2, 3)]  4.51 us
    pallas_call x2, Pallas kernels, tile_sums(): pl.pallas_call(lambda *refs: tile_kernel(which, *refs), out_shape=(jax.Sh...  3.96 us
    ppermute x2, starting transfers between devices, on_device(): came_odd = lax.ppermute(odd_ones, 'z', ODD_PAIRS)  3.68 us
    pallas_call x1, Pallas kernels, make_lists(): pl.pallas_call(list_kernel, out_shape=(pltpu.SMEM((ROOM + GROUP,), jnp.in...  3.44 us
  transfers between devices with their start and end apart: 22, of which 8 were waited for; matrix products, arithmetic and copies ran while one was open for 7% of the time, Pallas kernels for 7%

profile of v2, /device:TPU:1, one launch (start us, length us, event | category | flops | bytes accessed | tf_op | source)
XLA Modules:
  0.0 79.6 jit_solution(17728336877676735737)
XLA Ops:
  0.6 0.0 copy-start
  0.7 1.0 %compare_select_fusion = bf16[64,1024]{1,0:T(8,128)(2,1)S(1)} fusion(bf16[64,1024]{1,0:T(8,128)(2,1)} %param.10, bf16[64,1024]{1,0:T(8,128)(2,1)} %param.11), kind=kLoop, calls=%fused_computation.38 | loop fusion | flops 131072 | bytes 393216 | tf_op jit(solution)/shard_map/jit(_where)/select_n | solution.py:196
  1.7 3.4 %collective-permute-start.3 = (bf16[64,1024]{1,0:T(8,128)(2,1)S(1)}, bf16[64,1024]{1,0:T(8,128)(2,1)S(1)}, u32[]{:S(2)}, u32[]{:S(2)}) collective-permute-start(bf16[64,1024]{1,0:T(8,128)(2,1)S(1)} %compare_select_fusion), channel_id=1, source_target_pairs={{0,3},{1,0},{2,1},{3,2},{4,7},{5,4},{6,5},{7,6},{8,11},{9,8},{10,9... | collective-permute-start | bytes 393224 | tf_op jit(solution)/shard_map/ppermute | solution.py:202
  5.1 0.5 collective-permute-start.2
  5.6 0.6 collective-permute-start.1
  6.2 0.3 convolution_bitcast_fusion
  6.5 1.3 %convolution_bitcast_fusion.1 = f32[256,64]{0,1:T(8,128)S(1)} fusion(bf16[64,1024]{1,0:T(8,128)(2,1)S(1)} %compare_select_fusion, bf16[256,1024]{1,0:T(8,128)(2,1)} %param.12), kind=kOutput, calls=%fused_computation.6 | convolution fusion | flops 33554432 | bytes 720896 | tf_op jit(solution)/shard_map/dot_general | solution.py:189
  7.9 1.6 %collective-permute-start = (f32[256,64]{0,1:T(8,128)S(1)}, f32[256,64]{0,1:T(8,128)S(1)}, u32[]{:S(2)}, u32[]{:S(2)}) collective-permute-start(f32[256,64]{0,1:T(8,128)S(1)} %fusion.20), channel_id=1, source_target_pairs={{0,8},{8,0},{1,9},{9,1},{2,10},{10,2},{3,11},{11,3},{4,12},{12,4},... | collective-permute-start | bytes 196616 | tf_op jit(solution)/shard_map/ppermute | solution.py:161
  10.1 0.7 convert_reduce_fusion.1
  11.5 0.2 convert_reduce_fusion
  11.7 0.8 constant_dynamic-slice_fusion
  12.5 0.1 fusion.31
  12.6 0.0 collective-permute-done
  12.6 0.0 collective-permute-done.3
  12.6 2.0 %collective-permute-done.1 = bf16[64,1024]{1,0:T(8,128)(2,1)S(1)} collective-permute-done((bf16[64,1024]{1,0:T(8,128)(2,1)S(1)}, bf16[64,1024]{1,0:T(8,128)(2,1)S(1)}, u32[]{:S(2)}, u32[]{:S(2)}) %collective-permute-start.1) | collective-permute-done | bytes 131104 | tf_op jit(solution)/shard_map/ppermute | solution.py:202
  14.6 0.3 fusion.3
  14.9 1.7 %collective-permute-start.4 = (f32[256,64]{0,1:T(8,128)S(1)}, f32[256,64]{0,1:T(8,128)S(1)}, u32[]{:S(2)}, u32[]{:S(2)}) collective-permute-start(f32[256,64]{0,1:T(8,128)S(1)} %fusion.22), channel_id=1, source_target_pairs={{0,32},{32,0},{64,96},{96,64},{128,160},{160,128},{192,224},{224,1... | collective-permute-start | bytes 196616 | tf_op jit(solution)/shard_map/ppermute | solution.py:166
  16.7 2.9 %collective-permute-start.5 = (bf16[8,64,128]{2,1,0:T(8,128)(2,1)S(1)}, bf16[8,64,128]{2,1,0:T(8,128)(2,1)S(1)}, u32[]{:S(2)}, u32[]{:S(2)}) collective-permute-start(bf16[8,64,128]{2,1,0:T(8,128)(2,1)S(1)} %bitcast_bitcast_fusion.refs_2_), channel_id=1, source_target_pairs={{0,4},{4,0},{1,5},{5,1},{2,6},{6,2},{3,7},{7,3},{8,12},{12,8},{9,1... | collective-permute-start | bytes 393224 | tf_op jit(solution)/shard_map/ppermute | solution.py:214
  20.3 0.1 concatenate.24.table_ref
  20.3 3.4 %shard_map.121 = (s32[280]{0:T(512)S(4)}, s32[3]{0:T(128)S(4)}, bf16[280,128,128]{2,1,0:T(8,128)(2,1)S(1)}) custom-call(s32[516]{0:T(1024)S(1)} %concatenate.24.table_ref, bf16[256,128,128]{2,1,0:T(8,128)(2,1)} %vals_ref.1), custom_call_target="tpu_custom_call" | custom-call | bytes 12582912 | tf_op jit(solution)/shard_map/pallas_call | solution.py:71
  23.8 0.0 collective-permute-done.4
  23.8 0.0 collective-permute-done.5.refs_3_
  23.8 1.9 %shard_map.123 = (bf16[64,64,128]{2,1,0:T(8,128)(2,1)S(1)}, bf16[64,64,128]{2,1,0:T(8,128)(2,1)S(1)}) custom-call(s32[280]{0:T(512)S(4)} %get-tuple-element.35.refs_0_, s32[3]{0:T(128)S(4)} %get-tuple-element.36.refs_1_, bf16[8,64,128]{2,1,0:T(8,128)(2,1)S(1)} %bitcast_bitcast_fusion.refs_2_, bf16[8,64,128]{2,1,0:T(8,128)(2,1)S(1)} %collective-permute-done.5.refs_3_, ...), custom_call_target="tpu_custom_call" | custom-call | flops 134217728 | bytes 4194304 | tf_op jit(solution)/shard_map/pallas_call | solution.py:121
  25.8 0.1 collective-permute-start.11
  25.9 0.5 collective-permute-start.6
  26.4 2.9 %collective-permute-start.7 = (f32[256,64]{0,1:T(8,128)S(1)}, f32[256,64]{0,1:T(8,128)S(1)}, u32[]{:S(2)}, u32[]{:S(2)}) collective-permute-start(f32[256,64]{0,1:T(8,128)S(1)} %add.262), channel_id=1, source_target_pairs={{0,64},{32,96},{64,0},{96,32},{128,192},{160,224},{192,128},{224,1... | collective-permute-start | bytes 196616 | tf_op jit(solution)/shard_map/ppermute | solution.py:166
  29.3 2.0 %shard_map.122 = (f32[64,64,128]{2,1,0:T(8,128)S(1)}, f32[64,64,128]{2,1,0:T(8,128)S(1)}) custom-call(s32[280]{0:T(512)S(4)} %get-tuple-element.35.refs_0_, s32[3]{0:T(128)S(4)} %get-tuple-element.36.refs_1_, bf16[8,64,128]{2,1,0:T(8,128)(2,1)S(1)} %bitcast_bitcast_fusion.refs_2_, bf16[8,64,128]{2,1,0:T(8,128)(2,1)S(1)} %collective-permute-done.5.refs_3_, ...), custom_call_target="tpu_custom_call" | custom-call | flops 134217728 | bytes 4194304 | tf_op jit(solution)/shard_map/pallas_call | solution.py:121
  31.3 0.1 collective-permute-done.7
  31.4 0.0 collective-permute-done.11
  31.5 0.3 convert_add_fusion
  31.8 0.1 slice.136
  31.9 2.1 %collective-permute-start.12 = (bf16[2,2,4,2,64,128]{5,4,3,2,1,0:T(8,128)(2,1)S(1)}, bf16[2,2,4,2,64,128]{5,4,3,2,1,0:T(8,128)(2,1)S(1)}, u32[]{:S(2)}, u32[]{:S(2)}) collective-permute-start(bf16[2,2,4,2,64,128]{5,4,3,2,1,0:T(8,128)(2,1)S(1)} %bitcast.79), channel_id=1, source_target_pairs={{0,16},{16,0},{1,17},{17,1},{2,18},{18,2},{3,19},{19,3},{4,20},{20... | collective-permute-start | bytes 1572872 | tf_op jit(solution)/shard_map/ppermute | solution.py:235
  34.0 0.0 collective-permute-done.6
  34.0 0.4 fusion.54
  34.5 0.1 collective-permute-start.9
  34.6 3.7 %collective-permute-start.10 = (bf16[2,4,2,64,128]{4,3,2,1,0:T(8,128)(2,1)S(1)}, bf16[2,4,2,64,128]{4,3,2,1,0:T(8,128)(2,1)S(1)}, u32[]{:S(2)}, u32[]{:S(2)}) collective-permute-start(bf16[2,4,2,64,128]{4,3,2,1,0:T(8,128)(2,1)S(1)} %get-tuple-element.50), channel_id=1, source_target_pairs={{0,224},{32,64},{64,32},{96,128},{128,96},{160,192},{192,160},{224... | collective-permute-start | bytes 786440 | tf_op jit(solution)/shard_map/ppermute | solution.py:240
  38.2 2.3 %collective-permute-start.8 = (f32[256,64]{0,1:T(8,128)S(1)}, f32[256,64]{0,1:T(8,128)S(1)}, u32[]{:S(2)}, u32[]{:S(2)}) collective-permute-start(f32[256,64]{0,1:T(8,128)S(1)} %add.264), channel_id=1, source_target_pairs={{0,128},{32,160},{64,192},{96,224},{128,0},{160,32},{192,64},{224,... | collective-permute-start | bytes 196616 | tf_op jit(solution)/shard_map/ppermute | solution.py:166
  40.5 0.1 slice.83
  40.6 7.4 %collective-permute-done.8 = f32[256,64]{0,1:T(8,128)S(1)} collective-permute-done((f32[256,64]{0,1:T(8,128)S(1)}, f32[256,64]{0,1:T(8,128)S(1)}, u32[]{:S(2)}, u32[]{:S(2)}) %collective-permute-start.8) | collective-permute-done | bytes 65568 | tf_op jit(solution)/shard_map/ppermute | solution.py:166
  48.0 0.0 collective-permute-done.9
  48.0 0.0 collective-permute-done.10
  48.0 0.2 convert_add_fusion.3
  48.3 0.2 fusion.53
  48.5 0.3 collective-permute-start.14
  48.8 2.0 %collective-permute-start.15 = (bf16[4,2,64,128]{3,2,1,0:T(8,128)(2,1)S(1)}, bf16[4,2,64,128]{3,2,1,0:T(8,128)(2,1)S(1)}, u32[]{:S(2)}, u32[]{:S(2)}) collective-permute-start(bf16[4,2,64,128]{3,2,1,0:T(8,128)(2,1)S(1)} %get-tuple-element.59), channel_id=1, source_target_pairs={{0,32},{32,0},{64,96},{96,64},{128,160},{160,128},{192,224},{224,1... | collective-permute-start | bytes 393224 | tf_op jit(solution)/shard_map/ppermute | solution.py:248
  50.8 0.6 collective-permute-start.13
  51.4 4.1 %collective-permute-done.13 = f32[256,64]{0,1:T(8,128)S(1)} collective-permute-done((f32[256,64]{0,1:T(8,128)S(1)}, f32[256,64]{0,1:T(8,128)S(1)}, u32[]{:S(2)}, u32[]{:S(2)}) %collective-permute-start.13) | collective-permute-done | bytes 65568 | tf_op jit(solution)/shard_map/ppermute | solution.py:166
  55.5 0.3 collective-permute-done.16
  55.8 0.0 collective-permute-done.14
  55.8 0.1 fusion.2
  55.9 0.1 fusion.1
  56.0 0.1 fusion
  56.1 0.4 collective-permute-start.17
  56.5 4.2 %collective-permute-start.19 = (bf16[4,2,64,128]{3,2,1,0:T(8,128)(2,1)S(1)}, bf16[4,2,64,128]{3,2,1,0:T(8,128)(2,1)S(1)}, u32[]{:S(2)}, u32[]{:S(2)}) collective-permute-start(bf16[4,2,64,128]{3,2,1,0:T(8,128)(2,1)S(1)} %get-tuple-element.77), channel_id=1, source_target_pairs={{0,128},{32,160},{64,192},{96,224},{128,0},{160,32},{192,64},{224,... | collective-permute-start | bytes 393224 | tf_op jit(solution)/shard_map/ppermute | solution.py:256
  60.7 2.9 %collective-permute-start.18 = (bf16[4,2,64,128]{3,2,1,0:T(8,128)(2,1)S(1)}, bf16[4,2,64,128]{3,2,1,0:T(8,128)(2,1)S(1)}, u32[]{:S(2)}, u32[]{:S(2)}) collective-permute-start(bf16[4,2,64,128]{3,2,1,0:T(8,128)(2,1)S(1)} %get-tuple-element.78), channel_id=1, source_target_pairs={{0,192},{32,224},{64,0},{96,32},{128,64},{160,96},{192,128},{224,1... | collective-permute-start | bytes 393224 | tf_op jit(solution)/shard_map/ppermute | solution.py:256
  63.6 0.3 collective-permute-start.20
  63.9 4.1 %collective-permute-done.19 = bf16[4,2,64,128]{3,2,1,0:T(8,128)(2,1)S(1)} collective-permute-done((bf16[4,2,64,128]{3,2,1,0:T(8,128)(2,1)S(1)}, bf16[4,2,64,128]{3,2,1,0:T(8,128)(2,1)S(1)}, u32[]{:S(2)}, u32[]{:S(2)}) %collective-permute-start.19) | collective-permute-done | bytes 131104 | tf_op jit(solution)/shard_map/ppermute | solution.py:256
  68.0 6.6 %collective-permute-done.18 = bf16[4,2,64,128]{3,2,1,0:T(8,128)(2,1)S(1)} collective-permute-done((bf16[4,2,64,128]{3,2,1,0:T(8,128)(2,1)S(1)}, bf16[4,2,64,128]{3,2,1,0:T(8,128)(2,1)S(1)}, u32[]{:S(2)}, u32[]{:S(2)}) %collective-permute-start.18) | collective-permute-done | bytes 131104 | tf_op jit(solution)/shard_map/ppermute | solution.py:256
  74.6 0.1 fusion.16
  74.7 0.2 copy.29
  74.8 3.2 %collective-permute-start.21 = (f32[256,64]{0,1:T(8,128)S(1)}, f32[256,64]{0,1:T(8,128)S(1)}, u32[]{:S(2)}, u32[]{:S(2)}) collective-permute-start(f32[256,64]{0,1:T(8,128)S(1)} %add.276), channel_id=1, source_target_pairs={{0,8},{8,0},{1,9},{9,1},{2,10},{10,2},{3,11},{11,3},{4,12},{12,4},... | collective-permute-start | bytes 196616 | tf_op jit(solution)/shard_map/ppermute | solution.py:172
  78.0 0.7 fusion.17
  78.7 0.2 collective-permute-done.21
  78.9 0.7 fusion.55
  (29 shorter events, 0.3 us)
Async XLA Ops:
  0.6 5.6 %copy-start = (bf16[256,1024]{1,0:T(8,128)(2,1)S(1)}, bf16[256,1024]{1,0:T(8,128)(2,1)}, u32[]{:S(2)}) copy-start(bf16[256,1024]{1,0:T(8,128)(2,1)} %param.13) | copy-start | bytes 1572868
  0.6 9.5 %copy-start.2 = (s32[256]{0:T(256)S(1)}, s32[256]{0:T(256)}, u32[]{:S(2)}) copy-start(s32[256]{0:T(256)} %param.17) | copy-start | bytes 3076
  0.7 9.5 %copy-start.3 = (s32[256]{0:T(256)S(1)}, s32[256]{0:T(256)}, u32[]{:S(2)}) copy-start(s32[256]{0:T(256)} %param.16) | copy-start | bytes 3076
  1.7 10.9 %collective-permute-start.3 = (bf16[64,1024]{1,0:T(8,128)(2,1)S(1)}, bf16[64,1024]{1,0:T(8,128)(2,1)S(1)}, u32[]{:S(2)}, u32[]{:S(2)}) collective-permute-start(bf16[64,1024]{1,0:T(8,128)(2,1)S(1)} %compare_select_fusion), channel_id=1, source_target_pairs={{0,3},{1,0},{2,1},{3,2},{4,7},{5,4},{6,5},{7,6},{8,11},{9,8},{10,9... | collective-permute-start | bytes 393224 | tf_op jit(solution)/shard_map/ppermute | solution.py:202
  5.1 7.5 %collective-permute-start.2 = (bf16[64,1024]{1,0:T(8,128)(2,1)S(1)}, bf16[64,1024]{1,0:T(8,128)(2,1)S(1)}, u32[]{:S(2)}, u32[]{:S(2)}) collective-permute-start(bf16[64,1024]{1,0:T(8,128)(2,1)S(1)} %compare_select_fusion), channel_id=1, source_target_pairs={{0,2},{1,3},{2,0},{3,1},{4,6},{5,7},{6,4},{7,5},{8,10},{9,11},{10,... | collective-permute-start | bytes 393224 | tf_op jit(solution)/shard_map/ppermute | solution.py:202
  5.6 9.0 %collective-permute-start.1 = (bf16[64,1024]{1,0:T(8,128)(2,1)S(1)}, bf16[64,1024]{1,0:T(8,128)(2,1)S(1)}, u32[]{:S(2)}, u32[]{:S(2)}) collective-permute-start(bf16[64,1024]{1,0:T(8,128)(2,1)S(1)} %compare_select_fusion), channel_id=1, source_target_pairs={{0,1},{1,2},{2,3},{3,0},{4,5},{5,6},{6,7},{7,4},{8,9},{9,10},{10,1... | collective-permute-start | bytes 393224 | tf_op jit(solution)/shard_map/ppermute | solution.py:202
  7.9 4.7 %collective-permute-start = (f32[256,64]{0,1:T(8,128)S(1)}, f32[256,64]{0,1:T(8,128)S(1)}, u32[]{:S(2)}, u32[]{:S(2)}) collective-permute-start(f32[256,64]{0,1:T(8,128)S(1)} %fusion.20), channel_id=1, source_target_pairs={{0,8},{8,0},{1,9},{9,1},{2,10},{10,2},{3,11},{11,3},{4,12},{12,4},... | collective-permute-start | bytes 196616 | tf_op jit(solution)/shard_map/ppermute | solution.py:161
  14.9 8.9 %collective-permute-start.4 = (f32[256,64]{0,1:T(8,128)S(1)}, f32[256,64]{0,1:T(8,128)S(1)}, u32[]{:S(2)}, u32[]{:S(2)}) collective-permute-start(f32[256,64]{0,1:T(8,128)S(1)} %fusion.22), channel_id=1, source_target_pairs={{0,32},{32,0},{64,96},{96,64},{128,160},{160,128},{192,224},{224,1... | collective-permute-start | bytes 196616 | tf_op jit(solution)/shard_map/ppermute | solution.py:166
  16.7 7.2 %collective-permute-start.5 = (bf16[8,64,128]{2,1,0:T(8,128)(2,1)S(1)}, bf16[8,64,128]{2,1,0:T(8,128)(2,1)S(1)}, u32[]{:S(2)}, u32[]{:S(2)}) collective-permute-start(bf16[8,64,128]{2,1,0:T(8,128)(2,1)S(1)} %bitcast_bitcast_fusion.refs_2_), channel_id=1, source_target_pairs={{0,4},{4,0},{1,5},{5,1},{2,6},{6,2},{3,7},{7,3},{8,12},{12,8},{9,1... | collective-permute-start | bytes 393224 | tf_op jit(solution)/shard_map/ppermute | solution.py:214
  25.8 5.7 %collective-permute-start.11 = (bf16[64,64,128]{2,1,0:T(8,128)(2,1)S(1)}, bf16[64,64,128]{2,1,0:T(8,128)(2,1)S(1)}, u32[]{:S(2)}, u32[]{:S(2)}) collective-permute-start(bf16[64,64,128]{2,1,0:T(8,128)(2,1)S(1)} %get-tuple-element.52), channel_id=1, source_target_pairs={{0,8},{8,0},{1,9},{9,1},{2,10},{10,2},{3,11},{11,3},{4,12},{12,4},... | collective-permute-start | bytes 3145736 | tf_op jit(solution)/shard_map/ppermute | solution.py:231
  25.9 8.1 %collective-permute-start.6 = (bf16[64,64,128]{2,1,0:T(8,128)(2,1)S(1)}, bf16[64,64,128]{2,1,0:T(8,128)(2,1)S(1)}, u32[]{:S(2)}, u32[]{:S(2)}) collective-permute-start(bf16[64,64,128]{2,1,0:T(8,128)(2,1)S(1)} %get-tuple-element.46), channel_id=1, source_target_pairs={{0,8},{8,0},{1,9},{9,1},{2,10},{10,2},{3,11},{11,3},{4,12},{12,4},... | collective-permute-start | bytes 3145736 | tf_op jit(solution)/shard_map/ppermute | solution.py:232
  26.4 5.1 %collective-permute-start.7 = (f32[256,64]{0,1:T(8,128)S(1)}, f32[256,64]{0,1:T(8,128)S(1)}, u32[]{:S(2)}, u32[]{:S(2)}) collective-permute-start(f32[256,64]{0,1:T(8,128)S(1)} %add.262), channel_id=1, source_target_pairs={{0,64},{32,96},{64,0},{96,32},{128,192},{160,224},{192,128},{224,1... | collective-permute-start | bytes 196616 | tf_op jit(solution)/shard_map/ppermute | solution.py:166
  31.8 8.7 %copy-start.1 = (f32[64,64,128]{2,1,0:T(8,128)}, f32[64,64,128]{2,1,0:T(8,128)S(1)}, u32[]{:S(2)}) copy-start(f32[64,64,128]{2,1,0:T(8,128)S(1)} %convert_add_fusion) | copy-start | bytes 6291460
  31.9 16.1 %collective-permute-start.12 = (bf16[2,2,4,2,64,128]{5,4,3,2,1,0:T(8,128)(2,1)S(1)}, bf16[2,2,4,2,64,128]{5,4,3,2,1,0:T(8,128)(2,1)S(1)}, u32[]{:S(2)}, u32[]{:S(2)}) collective-permute-start(bf16[2,2,4,2,64,128]{5,4,3,2,1,0:T(8,128)(2,1)S(1)} %bitcast.79), channel_id=1, source_target_pairs={{0,16},{16,0},{1,17},{17,1},{2,18},{18,2},{3,19},{19,3},{4,20},{20... | collective-permute-start | bytes 1572872 | tf_op jit(solution)/shard_map/ppermute | solution.py:235
  34.5 13.5 %collective-permute-start.9 = (bf16[2,4,2,64,128]{4,3,2,1,0:T(8,128)(2,1)S(1)}, bf16[2,4,2,64,128]{4,3,2,1,0:T(8,128)(2,1)S(1)}, u32[]{:S(2)}, u32[]{:S(2)}) collective-permute-start(bf16[2,4,2,64,128]{4,3,2,1,0:T(8,128)(2,1)S(1)} %get-tuple-element.49), channel_id=1, source_target_pairs={{0,32},{32,0},{64,96},{96,64},{128,160},{160,128},{192,224},{224,1... | collective-permute-start | bytes 786440 | tf_op jit(solution)/shard_map/ppermute | solution.py:239
  34.6 13.4 %collective-permute-start.10 = (bf16[2,4,2,64,128]{4,3,2,1,0:T(8,128)(2,1)S(1)}, bf16[2,4,2,64,128]{4,3,2,1,0:T(8,128)(2,1)S(1)}, u32[]{:S(2)}, u32[]{:S(2)}) collective-permute-start(bf16[2,4,2,64,128]{4,3,2,1,0:T(8,128)(2,1)S(1)} %get-tuple-element.50), channel_id=1, source_target_pairs={{0,224},{32,64},{64,32},{96,128},{128,96},{160,192},{192,160},{224... | collective-permute-start | bytes 786440 | tf_op jit(solution)/shard_map/ppermute | solution.py:240
  38.2 9.7 %collective-permute-start.8 = (f32[256,64]{0,1:T(8,128)S(1)}, f32[256,64]{0,1:T(8,128)S(1)}, u32[]{:S(2)}, u32[]{:S(2)}) collective-permute-start(f32[256,64]{0,1:T(8,128)S(1)} %add.264), channel_id=1, source_target_pairs={{0,128},{32,160},{64,192},{96,224},{128,0},{160,32},{192,64},{224,... | collective-permute-start | bytes 196616 | tf_op jit(solution)/shard_map/ppermute | solution.py:166
  40.6 7.7 %slice-start = ((f32[64,64,128]{2,1,0:T(8,128)}), f32[32,64,128]{2,1,0:T(8,128)S(1)}, s32[]{:S(2)}) async-start(f32[64,64,128]{2,1,0:T(8,128)} %copy-done.1), calls=%async_computation | async-start | bytes 2097152 | tf_op jit(solution)/shard_map/slice | solution.py:244
  48.5 7.3 %collective-permute-start.14 = (bf16[2,4,2,64,128]{4,3,2,1,0:T(8,128)(2,1)S(1)}, bf16[2,4,2,64,128]{4,3,2,1,0:T(8,128)(2,1)S(1)}, u32[]{:S(2)}, u32[]{:S(2)}) collective-permute-start(bf16[2,4,2,64,128]{4,3,2,1,0:T(8,128)(2,1)S(1)} %fusion.11), channel_id=1, source_target_pairs={{0,16},{16,0},{1,17},{17,1},{2,18},{18,2},{3,19},{19,3},{4,20},{20... | collective-permute-start | bytes 786440 | tf_op jit(solution)/shard_map/ppermute | solution.py:247
  48.8 6.7 %collective-permute-start.15 = (bf16[4,2,64,128]{3,2,1,0:T(8,128)(2,1)S(1)}, bf16[4,2,64,128]{3,2,1,0:T(8,128)(2,1)S(1)}, u32[]{:S(2)}, u32[]{:S(2)}) collective-permute-start(bf16[4,2,64,128]{3,2,1,0:T(8,128)(2,1)S(1)} %get-tuple-element.59), channel_id=1, source_target_pairs={{0,32},{32,0},{64,96},{96,64},{128,160},{160,128},{192,224},{224,1... | collective-permute-start | bytes 393224 | tf_op jit(solution)/shard_map/ppermute | solution.py:248
  50.8 5.0 %collective-permute-start.16 = (bf16[4,2,64,128]{3,2,1,0:T(8,128)(2,1)S(1)}, bf16[4,2,64,128]{3,2,1,0:T(8,128)(2,1)S(1)}, u32[]{:S(2)}, u32[]{:S(2)}) collective-permute-start(bf16[4,2,64,128]{3,2,1,0:T(8,128)(2,1)S(1)} %get-tuple-element.60), channel_id=1, source_target_pairs={{0,224},{32,64},{64,32},{96,128},{128,96},{160,192},{192,160},{224... | collective-permute-start | bytes 393224 | tf_op jit(solution)/shard_map/ppermute | solution.py:249
  50.8 4.7 %collective-permute-start.13 = (f32[256,64]{0,1:T(8,128)S(1)}, f32[256,64]{0,1:T(8,128)S(1)}, u32[]{:S(2)}, u32[]{:S(2)}) collective-permute-start(f32[256,64]{0,1:T(8,128)S(1)} %add.265), channel_id=1, source_target_pairs={{0,16},{16,0},{1,17},{17,1},{2,18},{18,2},{3,19},{19,3},{4,20},{20... | collective-permute-start | bytes 196616 | tf_op jit(solution)/shard_map/ppermute | solution.py:166
  56.1 7.5 %collective-permute-start.17 = (bf16[4,2,64,128]{3,2,1,0:T(8,128)(2,1)S(1)}, bf16[4,2,64,128]{3,2,1,0:T(8,128)(2,1)S(1)}, u32[]{:S(2)}, u32[]{:S(2)}) collective-permute-start(bf16[4,2,64,128]{3,2,1,0:T(8,128)(2,1)S(1)} %get-tuple-element.76), channel_id=1, source_target_pairs={{0,64},{32,96},{64,128},{96,160},{128,192},{160,224},{192,0},{224,... | collective-permute-start | bytes 393224 | tf_op jit(solution)/shard_map/ppermute | solution.py:256
  56.5 11.5 %collective-permute-start.19 = (bf16[4,2,64,128]{3,2,1,0:T(8,128)(2,1)S(1)}, bf16[4,2,64,128]{3,2,1,0:T(8,128)(2,1)S(1)}, u32[]{:S(2)}, u32[]{:S(2)}) collective-permute-start(bf16[4,2,64,128]{3,2,1,0:T(8,128)(2,1)S(1)} %get-tuple-element.77), channel_id=1, source_target_pairs={{0,128},{32,160},{64,192},{96,224},{128,0},{160,32},{192,64},{224,... | collective-permute-start | bytes 393224 | tf_op jit(solution)/shard_map/ppermute | solution.py:256
  60.7 13.9 %collective-permute-start.18 = (bf16[4,2,64,128]{3,2,1,0:T(8,128)(2,1)S(1)}, bf16[4,2,64,128]{3,2,1,0:T(8,128)(2,1)S(1)}, u32[]{:S(2)}, u32[]{:S(2)}) collective-permute-start(bf16[4,2,64,128]{3,2,1,0:T(8,128)(2,1)S(1)} %get-tuple-element.78), channel_id=1, source_target_pairs={{0,192},{32,224},{64,0},{96,32},{128,64},{160,96},{192,128},{224,1... | collective-permute-start | bytes 393224 | tf_op jit(solution)/shard_map/ppermute | solution.py:256
  63.6 11.2 %collective-permute-start.20 = (f32[256,64]{0,1:T(8,128)S(1)}, f32[256,64]{0,1:T(8,128)S(1)}, u32[]{:S(2)}, u32[]{:S(2)}) collective-permute-start(f32[256,64]{0,1:T(8,128)S(1)} %add.269), channel_id=1, source_target_pairs={{0,4},{4,0},{1,5},{5,1},{2,6},{6,2},{3,7},{7,3},{8,12},{12,8},{9,1... | collective-permute-start | bytes 196616 | tf_op jit(solution)/shard_map/ppermute | solution.py:166
  74.8 4.1 %collective-permute-start.21 = (f32[256,64]{0,1:T(8,128)S(1)}, f32[256,64]{0,1:T(8,128)S(1)}, u32[]{:S(2)}, u32[]{:S(2)}) collective-permute-start(f32[256,64]{0,1:T(8,128)S(1)} %add.276), channel_id=1, source_target_pairs={{0,8},{8,0},{1,9},{9,1},{2,10},{10,2},{3,11},{11,3},{4,12},{12,4},... | collective-permute-start | bytes 196616 | tf_op jit(solution)/shard_map/ppermute | solution.py:172

commit v3 on v2

--- a/solution.py
+++ b/solution.py
@@ -165,17 +165,8 @@
     def join(axis, k):
         return lambda part: part + lax.ppermute(part, axis, [(i, i ^ k) for i in range(lax.axis_size(axis))])
 
-    def collect(axis):
-        me = lax.axis_index(axis)
-
-        def step(part):
-            came = lax.ppermute(part, axis, swap(2))
-            return jnp.where(me == 0, jnp.concatenate([part, came]), jnp.concatenate([came, part]))
-
-        return step
-
     return iter(
-        [give("core"), join("z", 1), join("z", 2), join("z", 4), join("pair", 1), join("half", 1), collect("core")]
+        [give("core"), join("z", 1), join("z", 4), join("z", 2), join("pair", 1), join("half", 1)]
     )
 
 
@@ -195,7 +186,6 @@
     z, pair, core, half, x = (lax.axis_index(a) for a in AXES)
     delta = jnp.where(preact > 0, cotangent, jnp.zeros_like(cotangent))
     rows, nodes = delta.shape
-    in_width = w_self.shape[0]
 
     steps = weight_steps()
     part = jnp.concatenate([contract_nodes(features, delta), contract_nodes(aggregated, delta)], axis=0)
@@ -235,7 +225,7 @@
     came_late = lax.ppermute(half16(late[1]), "pair", swap(2))
     early = under(early + wide(came_early), (2, 2, 2, 4, 2))
     even, odd_ones = half16(early[1, 0]), half16(early[1, 1])
-    part, even, odd_ones = beside(steps, 1, part, even, odd_ones)
+    part, even, odd_ones = lax.optimization_barrier((part, even, odd_ones))
     came_even = lax.ppermute(even, "z", EVEN_PAIRS)
     came_odd = lax.ppermute(odd_ones, "z", ODD_PAIRS)
     part, came_even, came_odd, came_late = beside(steps, 1, part, came_even, came_odd, came_late)
@@ -253,14 +243,15 @@
     late = late[:, 0] + wide(jnp.stack([came_even, came_odd]))
     both = jnp.concatenate([early, late], axis=0)
     rounded = half16(both)
+    part, rounded = lax.optimization_barrier((part, rounded))
     came = [lax.ppermute(rounded[:, k], "z", turn(2 * k, 8)) for k in (1, 3, 2)]
-    part, came[0] = lax.optimization_barrier((part, came[0]))
-    for step in steps:
-        part = step(part)
+    part = next(steps)(next(steps)(part))
+    other = lax.ppermute(part, "core", swap(2))
+    grads = jnp.where(core == 0, part, other), jnp.where(core == 0, other, part)
     summed = both[:, 0] + wide(came[0]) + wide(came[1]) + wide(came[2])
     summed = summed.reshape(8, rows, BLOCK).transpose(1, 0, 2).reshape(rows, nodes)
     input_grad = half16(summed + self_term)
-    return (input_grad, part[:in_width], part[in_width:])
+    return (input_grad, *grads)
 
 
 def solution(mesh):

time: 80.3 us -> 75.1 us (0.935)
  the two profiles are of different devices: /device:TPU:1 before, /device:TPU:32 now
where the time goes in v3:
time: 75.1 us; the launch traced here: 74.7 us
  starting transfers between devices  35 us (47%)
  waiting for transfers between devices  24.6 us (33%)
  other arithmetic  4.84 us (6%)
  Pallas kernels  3.91 us (5%)
  between operations  3.09 us (4%)
  matrix products  1.88 us (3%)
  local copies, waits for them, and re-layouts  1.35 us (2%)
    ppermute x5, waiting for transfers between devices, join(): lax.ppermute(part, axis, [(i, i ^ k) for i in range(lax.axis_size(axis))])  15.6 us
    ppermute x5, starting transfers between devices, join(): lax.ppermute(part, axis, [(i, i ^ k) for i in range(lax.axis_size(axis))])  8.3 us
    ppermute x3, starting transfers between devices, on_device(): came = [lax.ppermute(rounded[:, k], 'z', turn(2 * k, 8)) for k in (1, 3, 2)]  7.07 us
    ppermute x2, starting transfers between devices, on_device(): came_odd = lax.ppermute(odd_ones, 'z', ODD_PAIRS)  5.43 us
    ppermute x3, starting transfers between devices, on_device(): hidden = [lax.ppermute(delta, 'x', turn(k, 4)) for k in (1, 2, 3)]  4.52 us
    ppermute x3, waiting for transfers between devices, on_device(): came = [lax.ppermute(rounded[:, k], 'z', turn(2 * k, 8)) for k in (1, 3, 2)]  4.21 us
    ppermute x2, starting transfers between devices, on_device(): came_even = lax.ppermute(even, 'z', EVEN_PAIRS)  3.33 us
    ppermute x1, starting transfers between devices, on_device(): far = lax.ppermute(near, 'half', swap(2))  3.19 us
  transfers between devices with their start and end apart: 22, of which 9 were waited for; matrix products, arithmetic and copies ran while one was open for 7% of the time, Pallas kernels for 4%

profile of v3, /device:TPU:32, one launch (start us, length us, event | category | flops | bytes accessed | tf_op | source)
XLA Modules:
  0.0 74.7 jit_solution(9861268179764557442)
XLA Ops:
  0.6 0.0 copy-start
  0.7 1.0 %compare_select_fusion = bf16[64,1024]{1,0:T(8,128)(2,1)S(1)} fusion(bf16[64,1024]{1,0:T(8,128)(2,1)} %param.10, bf16[64,1024]{1,0:T(8,128)(2,1)} %param.11), kind=kLoop, calls=%fused_computation.38 | loop fusion | flops 131072 | bytes 393216 | tf_op jit(solution)/shard_map/jit(_where)/select_n | solution.py:187
  1.7 2.8 %collective-permute-start.3 = (bf16[64,1024]{1,0:T(8,128)(2,1)S(1)}, bf16[64,1024]{1,0:T(8,128)(2,1)S(1)}, u32[]{:S(2)}, u32[]{:S(2)}) collective-permute-start(bf16[64,1024]{1,0:T(8,128)(2,1)S(1)} %compare_select_fusion), channel_id=1, source_target_pairs={{0,3},{1,0},{2,1},{3,2},{4,7},{5,4},{6,5},{7,6},{8,11},{9,8},{10,9... | collective-permute-start | bytes 393224 | tf_op jit(solution)/shard_map/ppermute | solution.py:192
  4.5 0.8 %collective-permute-start.2 = (bf16[64,1024]{1,0:T(8,128)(2,1)S(1)}, bf16[64,1024]{1,0:T(8,128)(2,1)S(1)}, u32[]{:S(2)}, u32[]{:S(2)}) collective-permute-start(bf16[64,1024]{1,0:T(8,128)(2,1)S(1)} %compare_select_fusion), channel_id=1, source_target_pairs={{0,2},{1,3},{2,0},{3,1},{4,6},{5,7},{6,4},{7,5},{8,10},{9,11},{10,... | collective-permute-start | bytes 393224 | tf_op jit(solution)/shard_map/ppermute | solution.py:192
  5.3 0.9 %collective-permute-start.1 = (bf16[64,1024]{1,0:T(8,128)(2,1)S(1)}, bf16[64,1024]{1,0:T(8,128)(2,1)S(1)}, u32[]{:S(2)}, u32[]{:S(2)}) collective-permute-start(bf16[64,1024]{1,0:T(8,128)(2,1)S(1)} %compare_select_fusion), channel_id=1, source_target_pairs={{0,1},{1,2},{2,3},{3,0},{4,5},{5,6},{6,7},{7,4},{8,9},{9,10},{10,1... | collective-permute-start | bytes 393224 | tf_op jit(solution)/shard_map/ppermute | solution.py:192
  6.2 0.3 convolution_bitcast_fusion
  6.5 1.3 %convolution_bitcast_fusion.1 = f32[256,64]{0,1:T(8,128)S(1)} fusion(bf16[64,1024]{1,0:T(8,128)(2,1)S(1)} %compare_select_fusion, bf16[256,1024]{1,0:T(8,128)(2,1)} %param.12), kind=kOutput, calls=%fused_computation.6 | convolution fusion | flops 33554432 | bytes 720896 | tf_op jit(solution)/shard_map/dot_general | solution.py:180
  7.9 0.1 collective-permute-start
  8.7 0.7 convert_reduce_fusion.1
  10.0 0.2 convert_reduce_fusion
  10.2 0.8 %constant_dynamic-slice_fusion = (bf16[64,256]{1,0:T(8,128)(2,1)S(1)}, bf16[64,256]{1,0:T(8,128)(2,1)S(1)}) fusion(bf16[256,256]{1,0:T(8,128)(2,1)} %param.14, s32[]{:T(128)S(6)} %select_n.173, bf16[256,256]{1,0:T(8,128)(2,1)} %param.15), kind=kLoop, calls=%fused_computation.74 | loop fusion | bytes 131076 | tf_op jit(solution)/shard_map/dynamic_slice | solution.py:196
  11.0 0.1 fusion.31
  11.1 0.0 collective-permute-done
  11.2 1.2 %collective-permute-done.2 = bf16[64,1024]{1,0:T(8,128)(2,1)S(1)} collective-permute-done((bf16[64,1024]{1,0:T(8,128)(2,1)S(1)}, bf16[64,1024]{1,0:T(8,128)(2,1)S(1)}, u32[]{:S(2)}, u32[]{:S(2)}) %collective-permute-start.2) | collective-permute-done | bytes 131104 | tf_op jit(solution)/shard_map/ppermute | solution.py:192
  12.4 1.4 %collective-permute-done.1 = bf16[64,1024]{1,0:T(8,128)(2,1)S(1)} collective-permute-done((bf16[64,1024]{1,0:T(8,128)(2,1)S(1)}, bf16[64,1024]{1,0:T(8,128)(2,1)S(1)}, u32[]{:S(2)}, u32[]{:S(2)}) %collective-permute-start.1) | collective-permute-done | bytes 131104 | tf_op jit(solution)/shard_map/ppermute | solution.py:192
  13.8 0.3 fusion.3
  14.1 0.2 collective-permute-start.4
  14.3 3.2 %collective-permute-start.5 = (bf16[8,64,128]{2,1,0:T(8,128)(2,1)S(1)}, bf16[8,64,128]{2,1,0:T(8,128)(2,1)S(1)}, u32[]{:S(2)}, u32[]{:S(2)}) collective-permute-start(bf16[8,64,128]{2,1,0:T(8,128)(2,1)S(1)} %bitcast_bitcast_fusion.refs_2_), channel_id=1, source_target_pairs={{0,4},{4,0},{1,5},{5,1},{2,6},{6,2},{3,7},{7,3},{8,12},{12,8},{9,1... | collective-permute-start | bytes 393224 | tf_op jit(solution)/shard_map/ppermute | solution.py:204
  18.2 0.1 concatenate.18.table_ref
  18.3 1.8 %shard_map.121 = (s32[280]{0:T(512)S(4)}, s32[3]{0:T(128)S(4)}, bf16[280,128,128]{2,1,0:T(8,128)(2,1)S(1)}) custom-call(s32[516]{0:T(1024)S(1)} %concatenate.18.table_ref, bf16[256,128,128]{2,1,0:T(8,128)(2,1)} %vals_ref.1), custom_call_target="tpu_custom_call" | custom-call | bytes 12582912 | tf_op jit(solution)/shard_map/pallas_call | solution.py:71
  20.1 0.9 %collective-permute-done.5.refs_3_ = bf16[8,64,128]{2,1,0:T(8,128)(2,1)S(1)} collective-permute-done((bf16[8,64,128]{2,1,0:T(8,128)(2,1)S(1)}, bf16[8,64,128]{2,1,0:T(8,128)(2,1)S(1)}, u32[]{:S(2)}, u32[]{:S(2)}) %collective-permute-start.5) | collective-permute-done | bytes 131104 | tf_op jit(solution)/shard_map/ppermute | solution.py:204
  21.0 1.1 %shard_map.123 = (bf16[64,64,128]{2,1,0:T(8,128)(2,1)S(1)}, bf16[64,64,128]{2,1,0:T(8,128)(2,1)S(1)}) custom-call(s32[280]{0:T(512)S(4)} %get-tuple-element.35.refs_0_, s32[3]{0:T(128)S(4)} %get-tuple-element.36.refs_1_, bf16[8,64,128]{2,1,0:T(8,128)(2,1)S(1)} %bitcast_bitcast_fusion.refs_2_, bf16[8,64,128]{2,1,0:T(8,128)(2,1)S(1)} %collective-permute-done.5.refs_3_, ...), custom_call_target="tpu_custom_call" | custom-call | flops 134217728 | bytes 4194304 | tf_op jit(solution)/shard_map/pallas_call | solution.py:121
  22.2 0.1 collective-permute-start.10
  22.3 0.5 collective-permute-start.6
  22.8 1.0 %shard_map.122 = (f32[64,64,128]{2,1,0:T(8,128)S(1)}, f32[64,64,128]{2,1,0:T(8,128)S(1)}) custom-call(s32[280]{0:T(512)S(4)} %get-tuple-element.35.refs_0_, s32[3]{0:T(128)S(4)} %get-tuple-element.36.refs_1_, bf16[8,64,128]{2,1,0:T(8,128)(2,1)S(1)} %bitcast_bitcast_fusion.refs_2_, bf16[8,64,128]{2,1,0:T(8,128)(2,1)S(1)} %collective-permute-done.5.refs_3_, ...), custom_call_target="tpu_custom_call" | custom-call | flops 134217728 | bytes 4194304 | tf_op jit(solution)/shard_map/pallas_call | solution.py:121
  23.8 1.2 %collective-permute-done.10 = bf16[64,64,128]{2,1,0:T(8,128)(2,1)S(1)} collective-permute-done((bf16[64,64,128]{2,1,0:T(8,128)(2,1)S(1)}, bf16[64,64,128]{2,1,0:T(8,128)(2,1)S(1)}, u32[]{:S(2)}, u32[]{:S(2)}) %collective-permute-start.10) | collective-permute-done | bytes 1048608 | tf_op jit(solution)/shard_map/ppermute | solution.py:221
  24.9 0.3 convert_add_fusion
  25.3 0.1 slice.125
  25.4 1.5 %collective-permute-start.11 = (bf16[2,2,4,2,64,128]{5,4,3,2,1,0:T(8,128)(2,1)S(1)}, bf16[2,2,4,2,64,128]{5,4,3,2,1,0:T(8,128)(2,1)S(1)}, u32[]{:S(2)}, u32[]{:S(2)}) collective-permute-start(bf16[2,2,4,2,64,128]{5,4,3,2,1,0:T(8,128)(2,1)S(1)} %bitcast.75), channel_id=1, source_target_pairs={{0,16},{16,0},{1,17},{17,1},{2,18},{18,2},{3,19},{19,3},{4,20},{20... | collective-permute-start | bytes 1572872 | tf_op jit(solution)/shard_map/ppermute | solution.py:225
  26.8 0.0 collective-permute-done.6
  26.8 0.4 fusion.54
  27.3 2.6 %collective-permute-start.8 = (bf16[2,4,2,64,128]{4,3,2,1,0:T(8,128)(2,1)S(1)}, bf16[2,4,2,64,128]{4,3,2,1,0:T(8,128)(2,1)S(1)}, u32[]{:S(2)}, u32[]{:S(2)}) collective-permute-start(bf16[2,4,2,64,128]{4,3,2,1,0:T(8,128)(2,1)S(1)} %get-tuple-element.49), channel_id=1, source_target_pairs={{0,32},{32,0},{64,96},{96,64},{128,160},{160,128},{192,224},{224,1... | collective-permute-start | bytes 786440 | tf_op jit(solution)/shard_map/ppermute | solution.py:229
  29.8 3.7 %collective-permute-start.9 = (bf16[2,4,2,64,128]{4,3,2,1,0:T(8,128)(2,1)S(1)}, bf16[2,4,2,64,128]{4,3,2,1,0:T(8,128)(2,1)S(1)}, u32[]{:S(2)}, u32[]{:S(2)}) collective-permute-start(bf16[2,4,2,64,128]{4,3,2,1,0:T(8,128)(2,1)S(1)} %get-tuple-element.50), channel_id=1, source_target_pairs={{0,224},{32,64},{64,32},{96,128},{128,96},{160,192},{192,160},{224... | collective-permute-start | bytes 786440 | tf_op jit(solution)/shard_map/ppermute | solution.py:230
  33.6 3.3 %collective-permute-start.7 = (f32[256,64]{0,1:T(8,128)S(1)}, f32[256,64]{0,1:T(8,128)S(1)}, u32[]{:S(2)}, u32[]{:S(2)}) collective-permute-start(f32[256,64]{0,1:T(8,128)S(1)} %add.262), channel_id=1, source_target_pairs={{0,128},{32,160},{64,192},{96,224},{128,0},{160,32},{192,64},{224,... | collective-permute-start | bytes 196616 | tf_op jit(solution)/shard_map/ppermute | solution.py:166
  36.9 0.1 slice.75
  36.9 0.0 slice-start
  36.9 7.9 %collective-permute-done.7 = f32[256,64]{0,1:T(8,128)S(1)} collective-permute-done((f32[256,64]{0,1:T(8,128)S(1)}, f32[256,64]{0,1:T(8,128)S(1)}, u32[]{:S(2)}, u32[]{:S(2)}) %collective-permute-start.7) | collective-permute-done | bytes 65568 | tf_op jit(solution)/shard_map/ppermute | solution.py:166
  44.8 0.0 collective-permute-done.8
  44.8 0.0 collective-permute-done.11
  44.8 0.2 convert_add_fusion.3
  45.1 0.2 fusion.53
  45.3 0.9 %collective-permute-start.13 = (bf16[2,4,2,64,128]{4,3,2,1,0:T(8,128)(2,1)S(1)}, bf16[2,4,2,64,128]{4,3,2,1,0:T(8,128)(2,1)S(1)}, u32[]{:S(2)}, u32[]{:S(2)}) collective-permute-start(bf16[2,4,2,64,128]{4,3,2,1,0:T(8,128)(2,1)S(1)} %fusion.11), channel_id=1, source_target_pairs={{0,16},{16,0},{1,17},{17,1},{2,18},{18,2},{3,19},{19,3},{4,20},{20... | collective-permute-start | bytes 786440 | tf_op jit(solution)/shard_map/ppermute | solution.py:237
  46.3 0.8 %collective-permute-start.14 = (bf16[4,2,64,128]{3,2,1,0:T(8,128)(2,1)S(1)}, bf16[4,2,64,128]{3,2,1,0:T(8,128)(2,1)S(1)}, u32[]{:S(2)}, u32[]{:S(2)}) collective-permute-start(bf16[4,2,64,128]{3,2,1,0:T(8,128)(2,1)S(1)} %get-tuple-element.59), channel_id=1, source_target_pairs={{0,32},{32,0},{64,96},{96,64},{128,160},{160,128},{192,224},{224,1... | collective-permute-start | bytes 393224 | tf_op jit(solution)/shard_map/ppermute | solution.py:238
  47.0 1.7 %collective-permute-start.15 = (bf16[4,2,64,128]{3,2,1,0:T(8,128)(2,1)S(1)}, bf16[4,2,64,128]{3,2,1,0:T(8,128)(2,1)S(1)}, u32[]{:S(2)}, u32[]{:S(2)}) collective-permute-start(bf16[4,2,64,128]{3,2,1,0:T(8,128)(2,1)S(1)} %get-tuple-element.60), channel_id=1, source_target_pairs={{0,224},{32,64},{64,32},{96,128},{128,96},{160,192},{192,160},{224... | collective-permute-start | bytes 393224 | tf_op jit(solution)/shard_map/ppermute | solution.py:239
  48.8 1.6 %collective-permute-start.12 = (f32[256,64]{0,1:T(8,128)S(1)}, f32[256,64]{0,1:T(8,128)S(1)}, u32[]{:S(2)}, u32[]{:S(2)}) collective-permute-start(f32[256,64]{0,1:T(8,128)S(1)} %add.264), channel_id=1, source_target_pairs={{0,64},{32,96},{64,0},{96,32},{128,192},{160,224},{192,128},{224,1... | collective-permute-start | bytes 196616 | tf_op jit(solution)/shard_map/ppermute | solution.py:166
  50.3 3.7 %collective-permute-done.12 = f32[256,64]{0,1:T(8,128)S(1)} collective-permute-done((f32[256,64]{0,1:T(8,128)S(1)}, f32[256,64]{0,1:T(8,128)S(1)}, u32[]{:S(2)}, u32[]{:S(2)}) %collective-permute-start.12) | collective-permute-done | bytes 65568 | tf_op jit(solution)/shard_map/ppermute | solution.py:166
  54.1 0.0 collective-permute-done.15
  54.1 0.0 collective-permute-done.13
  54.1 0.1 fusion.2
  54.1 0.1 fusion.1
  54.2 0.1 fusion
  54.3 3.0 %collective-permute-start.19 = (f32[256,64]{0,1:T(8,128)S(1)}, f32[256,64]{0,1:T(8,128)S(1)}, u32[]{:S(2)}, u32[]{:S(2)}) collective-permute-start(f32[256,64]{0,1:T(8,128)S(1)} %add.268), channel_id=1, source_target_pairs={{0,4},{4,0},{1,5},{5,1},{2,6},{6,2},{3,7},{7,3},{8,12},{12,8},{9,1... | collective-permute-start | bytes 196616 | tf_op jit(solution)/shard_map/ppermute | solution.py:166
  57.3 2.3 %collective-permute-start.16 = (bf16[4,2,64,128]{3,2,1,0:T(8,128)(2,1)S(1)}, bf16[4,2,64,128]{3,2,1,0:T(8,128)(2,1)S(1)}, u32[]{:S(2)}, u32[]{:S(2)}) collective-permute-start(bf16[4,2,64,128]{3,2,1,0:T(8,128)(2,1)S(1)} %get-tuple-element.76), channel_id=1, source_target_pairs={{0,64},{32,96},{64,128},{96,160},{128,192},{160,224},{192,0},{224,... | collective-permute-start | bytes 393224 | tf_op jit(solution)/shard_map/ppermute | solution.py:247
  59.6 1.9 %collective-permute-start.17 = (bf16[4,2,64,128]{3,2,1,0:T(8,128)(2,1)S(1)}, bf16[4,2,64,128]{3,2,1,0:T(8,128)(2,1)S(1)}, u32[]{:S(2)}, u32[]{:S(2)}) collective-permute-start(bf16[4,2,64,128]{3,2,1,0:T(8,128)(2,1)S(1)} %get-tuple-element.77), channel_id=1, source_target_pairs={{0,192},{32,224},{64,0},{96,32},{128,64},{160,96},{192,128},{224,1... | collective-permute-start | bytes 393224 | tf_op jit(solution)/shard_map/ppermute | solution.py:247
  61.5 2.9 %collective-permute-start.18 = (bf16[4,2,64,128]{3,2,1,0:T(8,128)(2,1)S(1)}, bf16[4,2,64,128]{3,2,1,0:T(8,128)(2,1)S(1)}, u32[]{:S(2)}, u32[]{:S(2)}) collective-permute-start(bf16[4,2,64,128]{3,2,1,0:T(8,128)(2,1)S(1)} %slice_bitcast_fusion.8), channel_id=1, source_target_pairs={{0,128},{32,160},{64,192},{96,224},{128,0},{160,32},{192,64},{224,... | collective-permute-start | bytes 393224 | tf_op jit(solution)/shard_map/ppermute | solution.py:247
  64.4 0.3 collective-permute-start.20
  64.7 4.1 %collective-permute-done.20 = f32[256,64]{0,1:T(8,128)S(1)} collective-permute-done((f32[256,64]{0,1:T(8,128)S(1)}, f32[256,64]{0,1:T(8,128)S(1)}, u32[]{:S(2)}, u32[]{:S(2)}) %collective-permute-start.20) | collective-permute-done | bytes 65568 | tf_op jit(solution)/shard_map/ppermute | solution.py:166
  68.8 0.1 collective-permute-start.21
  68.9 0.1 collective-permute-done.16
  69.0 4.1 %collective-permute-done.18 = bf16[4,2,64,128]{3,2,1,0:T(8,128)(2,1)S(1)} collective-permute-done((bf16[4,2,64,128]{3,2,1,0:T(8,128)(2,1)S(1)}, bf16[4,2,64,128]{3,2,1,0:T(8,128)(2,1)S(1)}, u32[]{:S(2)}, u32[]{:S(2)}) %collective-permute-start.18) | collective-permute-done | bytes 131104 | tf_op jit(solution)/shard_map/ppermute | solution.py:247
  73.1 0.1 fusion.16
  73.1 0.2 copy.29
  73.3 0.7 fusion.17
  74.0 0.7 broadcast_select_fusion
  (29 shorter events, 0.3 us)
Async XLA Ops:
  0.6 5.6 %copy-start = (bf16[256,1024]{1,0:T(8,128)(2,1)S(1)}, bf16[256,1024]{1,0:T(8,128)(2,1)}, u32[]{:S(2)}) copy-start(bf16[256,1024]{1,0:T(8,128)(2,1)} %param.13) | copy-start | bytes 1572868
  0.6 8.0 %copy-start.2 = (s32[256]{0:T(256)S(1)}, s32[256]{0:T(256)}, u32[]{:S(2)}) copy-start(s32[256]{0:T(256)} %param.17) | copy-start | bytes 3076
  0.7 8.0 %copy-start.3 = (s32[256]{0:T(256)S(1)}, s32[256]{0:T(256)}, u32[]{:S(2)}) copy-start(s32[256]{0:T(256)} %param.16) | copy-start | bytes 3076
  1.7 9.5 %collective-permute-start.3 = (bf16[64,1024]{1,0:T(8,128)(2,1)S(1)}, bf16[64,1024]{1,0:T(8,128)(2,1)S(1)}, u32[]{:S(2)}, u32[]{:S(2)}) collective-permute-start(bf16[64,1024]{1,0:T(8,128)(2,1)S(1)} %compare_select_fusion), channel_id=1, source_target_pairs={{0,3},{1,0},{2,1},{3,2},{4,7},{5,4},{6,5},{7,6},{8,11},{9,8},{10,9... | collective-permute-start | bytes 393224 | tf_op jit(solution)/shard_map/ppermute | solution.py:192
  4.5 7.9 %collective-permute-start.2 = (bf16[64,1024]{1,0:T(8,128)(2,1)S(1)}, bf16[64,1024]{1,0:T(8,128)(2,1)S(1)}, u32[]{:S(2)}, u32[]{:S(2)}) collective-permute-start(bf16[64,1024]{1,0:T(8,128)(2,1)S(1)} %compare_select_fusion), channel_id=1, source_target_pairs={{0,2},{1,3},{2,0},{3,1},{4,6},{5,7},{6,4},{7,5},{8,10},{9,11},{10,... | collective-permute-start | bytes 393224 | tf_op jit(solution)/shard_map/ppermute | solution.py:192
  5.3 8.5 %collective-permute-start.1 = (bf16[64,1024]{1,0:T(8,128)(2,1)S(1)}, bf16[64,1024]{1,0:T(8,128)(2,1)S(1)}, u32[]{:S(2)}, u32[]{:S(2)}) collective-permute-start(bf16[64,1024]{1,0:T(8,128)(2,1)S(1)} %compare_select_fusion), channel_id=1, source_target_pairs={{0,1},{1,2},{2,3},{3,0},{4,5},{5,6},{6,7},{7,4},{8,9},{9,10},{10,1... | collective-permute-start | bytes 393224 | tf_op jit(solution)/shard_map/ppermute | solution.py:192
  7.9 3.3 %collective-permute-start = (f32[256,64]{0,1:T(8,128)S(1)}, f32[256,64]{0,1:T(8,128)S(1)}, u32[]{:S(2)}, u32[]{:S(2)}) collective-permute-start(f32[256,64]{0,1:T(8,128)S(1)} %fusion.20), channel_id=1, source_target_pairs={{0,8},{8,0},{1,9},{9,1},{2,10},{10,2},{3,11},{11,3},{4,12},{12,4},... | collective-permute-start | bytes 196616 | tf_op jit(solution)/shard_map/ppermute | solution.py:161
  14.1 6.0 %collective-permute-start.4 = (f32[256,64]{0,1:T(8,128)S(1)}, f32[256,64]{0,1:T(8,128)S(1)}, u32[]{:S(2)}, u32[]{:S(2)}) collective-permute-start(f32[256,64]{0,1:T(8,128)S(1)} %fusion.22), channel_id=1, source_target_pairs={{0,32},{32,0},{64,96},{96,64},{128,160},{160,128},{192,224},{224,1... | collective-permute-start | bytes 196616 | tf_op jit(solution)/shard_map/ppermute | solution.py:166
  14.3 6.7 %collective-permute-start.5 = (bf16[8,64,128]{2,1,0:T(8,128)(2,1)S(1)}, bf16[8,64,128]{2,1,0:T(8,128)(2,1)S(1)}, u32[]{:S(2)}, u32[]{:S(2)}) collective-permute-start(bf16[8,64,128]{2,1,0:T(8,128)(2,1)S(1)} %bitcast_bitcast_fusion.refs_2_), channel_id=1, source_target_pairs={{0,4},{4,0},{1,5},{5,1},{2,6},{6,2},{3,7},{7,3},{8,12},{12,8},{9,1... | collective-permute-start | bytes 393224 | tf_op jit(solution)/shard_map/ppermute | solution.py:204
  22.2 2.7 %collective-permute-start.10 = (bf16[64,64,128]{2,1,0:T(8,128)(2,1)S(1)}, bf16[64,64,128]{2,1,0:T(8,128)(2,1)S(1)}, u32[]{:S(2)}, u32[]{:S(2)}) collective-permute-start(bf16[64,64,128]{2,1,0:T(8,128)(2,1)S(1)} %get-tuple-element.52), channel_id=1, source_target_pairs={{0,8},{8,0},{1,9},{9,1},{2,10},{10,2},{3,11},{11,3},{4,12},{12,4},... | collective-permute-start | bytes 3145736 | tf_op jit(solution)/shard_map/ppermute | solution.py:221
  22.3 4.5 %collective-permute-start.6 = (bf16[64,64,128]{2,1,0:T(8,128)(2,1)S(1)}, bf16[64,64,128]{2,1,0:T(8,128)(2,1)S(1)}, u32[]{:S(2)}, u32[]{:S(2)}) collective-permute-start(bf16[64,64,128]{2,1,0:T(8,128)(2,1)S(1)} %get-tuple-element.46), channel_id=1, source_target_pairs={{0,8},{8,0},{1,9},{9,1},{2,10},{10,2},{3,11},{11,3},{4,12},{12,4},... | collective-permute-start | bytes 3145736 | tf_op jit(solution)/shard_map/ppermute | solution.py:222
  25.3 11.6 %copy-start.1 = (f32[64,64,128]{2,1,0:T(8,128)}, f32[64,64,128]{2,1,0:T(8,128)S(1)}, u32[]{:S(2)}) copy-start(f32[64,64,128]{2,1,0:T(8,128)S(1)} %convert_add_fusion) | copy-start | bytes 6291460
  25.4 19.5 %collective-permute-start.11 = (bf16[2,2,4,2,64,128]{5,4,3,2,1,0:T(8,128)(2,1)S(1)}, bf16[2,2,4,2,64,128]{5,4,3,2,1,0:T(8,128)(2,1)S(1)}, u32[]{:S(2)}, u32[]{:S(2)}) collective-permute-start(bf16[2,2,4,2,64,128]{5,4,3,2,1,0:T(8,128)(2,1)S(1)} %bitcast.75), channel_id=1, source_target_pairs={{0,16},{16,0},{1,17},{17,1},{2,18},{18,2},{3,19},{19,3},{4,20},{20... | collective-permute-start | bytes 1572872 | tf_op jit(solution)/shard_map/ppermute | solution.py:225
  27.3 17.5 %collective-permute-start.8 = (bf16[2,4,2,64,128]{4,3,2,1,0:T(8,128)(2,1)S(1)}, bf16[2,4,2,64,128]{4,3,2,1,0:T(8,128)(2,1)S(1)}, u32[]{:S(2)}, u32[]{:S(2)}) collective-permute-start(bf16[2,4,2,64,128]{4,3,2,1,0:T(8,128)(2,1)S(1)} %get-tuple-element.49), channel_id=1, source_target_pairs={{0,32},{32,0},{64,96},{96,64},{128,160},{160,128},{192,224},{224,1... | collective-permute-start | bytes 786440 | tf_op jit(solution)/shard_map/ppermute | solution.py:229
  29.8 15.0 %collective-permute-start.9 = (bf16[2,4,2,64,128]{4,3,2,1,0:T(8,128)(2,1)S(1)}, bf16[2,4,2,64,128]{4,3,2,1,0:T(8,128)(2,1)S(1)}, u32[]{:S(2)}, u32[]{:S(2)}) collective-permute-start(bf16[2,4,2,64,128]{4,3,2,1,0:T(8,128)(2,1)S(1)} %get-tuple-element.50), channel_id=1, source_target_pairs={{0,224},{32,64},{64,32},{96,128},{128,96},{160,192},{192,160},{224... | collective-permute-start | bytes 786440 | tf_op jit(solution)/shard_map/ppermute | solution.py:230
  33.6 11.2 %collective-permute-start.7 = (f32[256,64]{0,1:T(8,128)S(1)}, f32[256,64]{0,1:T(8,128)S(1)}, u32[]{:S(2)}, u32[]{:S(2)}) collective-permute-start(f32[256,64]{0,1:T(8,128)S(1)} %add.262), channel_id=1, source_target_pairs={{0,128},{32,160},{64,192},{96,224},{128,0},{160,32},{192,64},{224,... | collective-permute-start | bytes 196616 | tf_op jit(solution)/shard_map/ppermute | solution.py:166
  36.9 8.1 %slice-start = ((f32[64,64,128]{2,1,0:T(8,128)}), f32[32,64,128]{2,1,0:T(8,128)S(1)}, s32[]{:S(2)}) async-start(f32[64,64,128]{2,1,0:T(8,128)} %copy-done.1), calls=%async_computation | async-start | bytes 2097152 | tf_op jit(solution)/shard_map/slice | solution.py:234
  45.3 8.7 %collective-permute-start.13 = (bf16[2,4,2,64,128]{4,3,2,1,0:T(8,128)(2,1)S(1)}, bf16[2,4,2,64,128]{4,3,2,1,0:T(8,128)(2,1)S(1)}, u32[]{:S(2)}, u32[]{:S(2)}) collective-permute-start(bf16[2,4,2,64,128]{4,3,2,1,0:T(8,128)(2,1)S(1)} %fusion.11), channel_id=1, source_target_pairs={{0,16},{16,0},{1,17},{17,1},{2,18},{18,2},{3,19},{19,3},{4,20},{20... | collective-permute-start | bytes 786440 | tf_op jit(solution)/shard_map/ppermute | solution.py:237
  46.3 7.8 %collective-permute-start.14 = (bf16[4,2,64,128]{3,2,1,0:T(8,128)(2,1)S(1)}, bf16[4,2,64,128]{3,2,1,0:T(8,128)(2,1)S(1)}, u32[]{:S(2)}, u32[]{:S(2)}) collective-permute-start(bf16[4,2,64,128]{3,2,1,0:T(8,128)(2,1)S(1)} %get-tuple-element.59), channel_id=1, source_target_pairs={{0,32},{32,0},{64,96},{96,64},{128,160},{160,128},{192,224},{224,1... | collective-permute-start | bytes 393224 | tf_op jit(solution)/shard_map/ppermute | solution.py:238
  47.0 7.0 %collective-permute-start.15 = (bf16[4,2,64,128]{3,2,1,0:T(8,128)(2,1)S(1)}, bf16[4,2,64,128]{3,2,1,0:T(8,128)(2,1)S(1)}, u32[]{:S(2)}, u32[]{:S(2)}) collective-permute-start(bf16[4,2,64,128]{3,2,1,0:T(8,128)(2,1)S(1)} %get-tuple-element.60), channel_id=1, source_target_pairs={{0,224},{32,64},{64,32},{96,128},{128,96},{160,192},{192,160},{224... | collective-permute-start | bytes 393224 | tf_op jit(solution)/shard_map/ppermute | solution.py:239
  48.8 5.3 %collective-permute-start.12 = (f32[256,64]{0,1:T(8,128)S(1)}, f32[256,64]{0,1:T(8,128)S(1)}, u32[]{:S(2)}, u32[]{:S(2)}) collective-permute-start(f32[256,64]{0,1:T(8,128)S(1)} %add.264), channel_id=1, source_target_pairs={{0,64},{32,96},{64,0},{96,32},{128,192},{160,224},{192,128},{224,1... | collective-permute-start | bytes 196616 | tf_op jit(solution)/shard_map/ppermute | solution.py:166
  54.3 10.1 %collective-permute-start.19 = (f32[256,64]{0,1:T(8,128)S(1)}, f32[256,64]{0,1:T(8,128)S(1)}, u32[]{:S(2)}, u32[]{:S(2)}) collective-permute-start(f32[256,64]{0,1:T(8,128)S(1)} %add.268), channel_id=1, source_target_pairs={{0,4},{4,0},{1,5},{5,1},{2,6},{6,2},{3,7},{7,3},{8,12},{12,8},{9,1... | collective-permute-start | bytes 196616 | tf_op jit(solution)/shard_map/ppermute | solution.py:166
  57.3 11.7 %collective-permute-start.16 = (bf16[4,2,64,128]{3,2,1,0:T(8,128)(2,1)S(1)}, bf16[4,2,64,128]{3,2,1,0:T(8,128)(2,1)S(1)}, u32[]{:S(2)}, u32[]{:S(2)}) collective-permute-start(bf16[4,2,64,128]{3,2,1,0:T(8,128)(2,1)S(1)} %get-tuple-element.76), channel_id=1, source_target_pairs={{0,64},{32,96},{64,128},{96,160},{128,192},{160,224},{192,0},{224,... | collective-permute-start | bytes 393224 | tf_op jit(solution)/shard_map/ppermute | solution.py:247
  59.6 9.4 %collective-permute-start.17 = (bf16[4,2,64,128]{3,2,1,0:T(8,128)(2,1)S(1)}, bf16[4,2,64,128]{3,2,1,0:T(8,128)(2,1)S(1)}, u32[]{:S(2)}, u32[]{:S(2)}) collective-permute-start(bf16[4,2,64,128]{3,2,1,0:T(8,128)(2,1)S(1)} %get-tuple-element.77), channel_id=1, source_target_pairs={{0,192},{32,224},{64,0},{96,32},{128,64},{160,96},{192,128},{224,1... | collective-permute-start | bytes 393224 | tf_op jit(solution)/shard_map/ppermute | solution.py:247
  61.5 11.6 %collective-permute-start.18 = (bf16[4,2,64,128]{3,2,1,0:T(8,128)(2,1)S(1)}, bf16[4,2,64,128]{3,2,1,0:T(8,128)(2,1)S(1)}, u32[]{:S(2)}, u32[]{:S(2)}) collective-permute-start(bf16[4,2,64,128]{3,2,1,0:T(8,128)(2,1)S(1)} %slice_bitcast_fusion.8), channel_id=1, source_target_pairs={{0,128},{32,160},{64,192},{96,224},{128,0},{160,32},{192,64},{224,... | collective-permute-start | bytes 393224 | tf_op jit(solution)/shard_map/ppermute | solution.py:247
  64.4 4.4 %collective-permute-start.20 = (f32[256,64]{0,1:T(8,128)S(1)}, f32[256,64]{0,1:T(8,128)S(1)}, u32[]{:S(2)}, u32[]{:S(2)}) collective-permute-start(f32[256,64]{0,1:T(8,128)S(1)} %add.275), channel_id=1, source_target_pairs={{0,16},{16,0},{1,17},{17,1},{2,18},{18,2},{3,19},{19,3},{4,20},{20... | collective-permute-start | bytes 196616 | tf_op jit(solution)/shard_map/ppermute | solution.py:166
  68.8 5.3 %collective-permute-start.21 = (f32[256,64]{0,1:T(8,128)S(1)}, f32[256,64]{0,1:T(8,128)S(1)}, u32[]{:S(2)}, u32[]{:S(2)}) collective-permute-start(f32[256,64]{0,1:T(8,128)S(1)} %add.276), channel_id=1, source_target_pairs={{0,8},{8,0},{1,9},{9,1},{2,10},{10,2},{3,11},{11,3},{4,12},{12,4},... | collective-permute-start | bytes 196616 | tf_op jit(solution)/shard_map/ppermute | solution.py:249

commit v4 on v3

--- a/solution.py
+++ b/solution.py
@@ -7,10 +7,11 @@
 
 AXES = ("z", "pair", "core", "half", "x")
 BLOCK = 128
-GROUP = 8
-BIG = 32
-LISTS = 2
-PLACES = 128
+GROUP = 16
+BIG = 64
+CHUNK = 32
+LISTS = 3
+PLACES = 64
 ROOM = 256 + LISTS * GROUP
 SCOPED = 16 * 1024 * 1024
 
@@ -29,51 +30,60 @@
 
 def list_kernel(table_ref, vals_ref, lists_ref, starts_ref, tiles_ref, sem):
     slots = vals_ref.shape[0]
-    steps = (table_ref[2 * slots + LISTS + 1] + GROUP - 1) // GROUP
+    live = table_ref[2 * slots + 8]
+    chunks = (live + CHUNK - 1) // CHUNK
+
+    def fetch(chunk, carry):
+        some = pl.ds(chunk * CHUNK, CHUNK)
+        pltpu.make_async_copy(vals_ref.at[some], tiles_ref.at[some], sem).start()
+        return carry
+
+    lax.fori_loop(0, chunks, fetch, 0)
     starts_ref[0] = table_ref[2 * slots]
     for i in range(1, LISTS + 1):
         end = table_ref[2 * slots + i]
         starts_ref[i] = end
         for k in range(GROUP - 1):
-            lists_ref[jnp.maximum(end - 1 - k, 0)] = jnp.int32(PLACES)
+            lists_ref[jnp.maximum(end - 1 - k, 0)] = jnp.int32(2 * PLACES)
 
     def place(step, carry):
         for k in range(GROUP):
             slot = step * GROUP + k
-            spot = table_ref[slot]
-            lists_ref[spot] = table_ref[slots + slot]
-            pltpu.make_async_copy(vals_ref.at[slot], tiles_ref.at[spot], sem).start()
-        return carry
-
-    def finish(step, carry):
-        some = pl.ds(0, GROUP)
+            lists_ref[table_ref[slot]] = table_ref[slots + slot]
+        return carry
+
+    def finish(chunk, carry):
+        some = pl.ds(0, CHUNK)
         pltpu.make_async_copy(vals_ref.at[some], tiles_ref.at[some], sem).wait()
         return carry
 
-    lax.fori_loop(0, steps, place, 0)
-    lax.fori_loop(0, steps, finish, 0)
-
-
-def make_lists(live, entries, which, vals):
-    slots = jnp.arange(vals.shape[0], dtype=jnp.int32)
+    lax.fori_loop(0, (live + GROUP - 1) // GROUP, place, 0)
+    lax.fori_loop(0, chunks, finish, 0)
+
+
+def list_table(live, entries, which):
+    slots = jnp.arange(entries.shape[0], dtype=jnp.int32)
     which = jnp.where(slots < live, which, LISTS)
     earlier = (which[:, None] == which[None, :]) & (slots[:, None] > slots[None, :])
     rank = jnp.sum(earlier.astype(jnp.int32), axis=1)
-    starts = [jnp.int32(0)]
-    for i in range(LISTS):
-        held = jnp.sum((which == i).astype(jnp.int32))
-        starts.append(starts[-1] + (held + GROUP - 1) // GROUP * GROUP)
-    spots = ROOM + slots % GROUP
-    for i in range(LISTS):
-        spots = jnp.where(which == i, starts[i] + rank, spots)
-    table = jnp.concatenate([spots, entries, jnp.stack(starts + [live])])
+    lists = jnp.arange(8, dtype=jnp.int32)
+    member = which[:, None] == lists[None, :]
+    held = jnp.sum(member.astype(jnp.int32), axis=0)
+    room = (held + GROUP - 1) // GROUP * GROUP
+    starts = jnp.sum(jnp.where(lists[:, None] < lists[None, :], room[:, None], 0), axis=0)
+    first = jnp.sum(jnp.where(member, starts[None, :], 0), axis=1)
+    spots = jnp.where(which < LISTS, first + rank, ROOM + slots % GROUP)
+    return jnp.concatenate([spots, slots * 65536 + entries, starts, live])
+
+
+def make_lists(table, vals):
     smem = pl.BlockSpec(memory_space=pltpu.SMEM)
     return pl.pallas_call(
         list_kernel,
         out_shape=(
             pltpu.SMEM((ROOM + GROUP,), jnp.int32),
             pltpu.SMEM((LISTS + 1,), jnp.int32),
-            pltpu.VMEM((ROOM + GROUP, BLOCK, BLOCK), vals.dtype),
+            pltpu.VMEM(vals.shape, vals.dtype),
         ),
         in_specs=[smem, pl.BlockSpec(memory_space=pl.ANY)],
         out_specs=(smem, smem, pl.BlockSpec(memory_space=pltpu.VMEM)),
@@ -83,17 +93,19 @@
     )(table, pltpu.with_memory_space_constraint(vals, pltpu.HBM))
 
 
-def tile_kernel(which, lists_ref, starts_ref, near_ref, far_ref, tiles_ref, first_ref, last_ref, total, panel):
+def tile_kernel(which, lists_ref, starts_ref, near_ref, far_ref, tiles_ref, *refs):
+    *outs, total, panel = refs
     start, end = starts_ref[which], starts_ref[which + 1]
     panel[0:8] = near_ref[...]
     panel[8:16] = far_ref[...]
-    total[...] = jnp.zeros_like(total)
+    used = len(outs) * PLACES
+    total[0:used] = jnp.zeros((used, *total.shape[1:]), total.dtype)
 
     def add(base, count):
         entries = [lists_ref[base + k] for k in range(count)]
         products = [
-            jnp.dot(panel[entry // 256], tiles_ref[base + k], preferred_element_type=jnp.float32)
-            for k, entry in enumerate(entries)
+            jnp.dot(panel[entry // 256 & 255], tiles_ref[entry // 65536], preferred_element_type=jnp.float32)
+            for entry in entries
         ]
         for entry, product in zip(entries, products):
             total[entry & 255] += product
@@ -102,29 +114,27 @@
         add(start + step * BIG, BIG)
         return carry
 
-    def small(step, carry):
-        add(start + step * GROUP, GROUP)
-        return carry
-
-    bigs = (end - start) // BIG
-    lax.fori_loop(0, bigs, big, 0)
-    lax.fori_loop(bigs * (BIG // GROUP), (end - start) // GROUP, small, 0)
-    n = PLACES // 2
-    first_ref[...] = total[0:n].astype(first_ref.dtype)
-    last_ref[...] = total[n : 2 * n].astype(last_ref.dtype)
-
-
-def tile_sums(which, lists, starts, near, far, tiles, dtype):
+    count = end - start
+    lax.fori_loop(0, count // BIG, big, 0)
+    size = BIG // 2
+    while size >= GROUP:
+        pl.when(count & size != 0)(lambda size=size: add(start + count // (2 * size) * (2 * size), size))
+        size //= 2
+    for i, out_ref in enumerate(outs):
+        out_ref[...] = total[i * PLACES : (i + 1) * PLACES].astype(out_ref.dtype)
+
+
+def tile_sums(which, outs, lists, starts, near, far, tiles, dtype):
     rows = near.shape[1]
     smem = pl.BlockSpec(memory_space=pltpu.SMEM)
     vmem = pl.BlockSpec(memory_space=pltpu.VMEM)
     return pl.pallas_call(
         lambda *refs: tile_kernel(which, *refs),
-        out_shape=(jax.ShapeDtypeStruct((PLACES // 2, rows, BLOCK), dtype),) * 2,
+        out_shape=(jax.ShapeDtypeStruct((PLACES, rows, BLOCK), dtype),) * outs,
         in_specs=[smem, smem, vmem, vmem, vmem],
-        out_specs=(vmem, vmem),
+        out_specs=(vmem,) * outs,
         scratch_shapes=[
-            pltpu.VMEM((PLACES + 1, rows, BLOCK), jnp.float32),
+            pltpu.VMEM((2 * PLACES + 1, rows, BLOCK), jnp.float32),
             pltpu.VMEM((16, rows, BLOCK), jnp.bfloat16),
         ],
         compiler_params=pltpu.CompilerParams(vmem_limit_bytes=SCOPED),
@@ -166,7 +176,7 @@
         return lambda part: part + lax.ppermute(part, axis, [(i, i ^ k) for i in range(lax.axis_size(axis))])
 
     return iter(
-        [give("core"), join("z", 1), join("z", 4), join("z", 2), join("pair", 1), join("half", 1)]
+        [give("core"), join("z", 1), join("z", 4), join("z", 2), join("half", 1), join("pair", 1)]
     )
 
 
@@ -189,22 +199,17 @@
 
     steps = weight_steps()
     part = jnp.concatenate([contract_nodes(features, delta), contract_nodes(aggregated, delta)], axis=0)
-    hidden = [lax.ppermute(delta, "x", turn(k, 4)) for k in (1, 2, 3)]
+    hidden = [lax.ppermute(delta, "x", turn(k, 4)) for k in (2, 3, 1)]
     part, *hidden = beside(steps, 1, part, *hidden)
     hidden = [delta] + hidden
     weights = jnp.concatenate(
         [lax.dynamic_slice_in_dim(w, x * rows, rows, 0) for w in (w_neigh, w_self)], axis=0
     )
     weights = jnp.concatenate(
-        [lax.dynamic_slice_in_dim(weights, (x + 4 - k) % 4 * rows, rows, 1) for k in range(4)], axis=1
+        [lax.dynamic_slice_in_dim(weights, (x + 4 - k) % 4 * rows, rows, 1) for k in (0, 2, 3, 1)], axis=1
     )
     both = jnp.dot(weights, jnp.concatenate(hidden, axis=0), preferred_element_type=jnp.float32)
     near = half16(both[:rows]).reshape(rows, nodes // BLOCK, BLOCK).transpose(1, 0, 2)
-    part, near = lax.optimization_barrier((part, near))
-    far = lax.ppermute(near, "half", swap(2))
-    part, far = beside(steps, 1, part, far)
-    self_term = both[rows:]
-
     owner, within = tile_cols // 16, tile_cols % 8
     late, odd = within // 4, within // 2 % 2
     at, me = (owner // 4 + odd) % 8, (z + odd) % 8
@@ -214,13 +219,24 @@
     place = jnp.where(late == 1, (across * 2 + odd) * 2 + step, (step * 2 + odd) * 2 + across)
     place = ((1 - late) * 8 + place) * 8 + turns * 2 + within % 2
     block = (tile_rows - (z * 4 + pair * 2 + core) * 16) ^ (half * 8)
-    which = 1 - ((owner % 2) ^ core).astype(jnp.int32)
-    lists, starts, tiles = make_lists(tile_live[0], block * 256 + place, which, tile_vals)
-
-    away_late, away_early = tile_sums(0, lists, starts, near, far, tiles, jnp.bfloat16)
-    came_late = lax.ppermute(away_late, "core", swap(2))
-    came_early = lax.ppermute(away_early, "core", swap(2))
-    late, early = tile_sums(1, lists, starts, near, far, tiles, jnp.float32)
+    which = jnp.where((owner % 2) ^ core == 1, 1 - late, 2)
+    place = place - jnp.where(which == 1, PLACES, 0)
+    table = list_table(tile_live, block * 256 + place, which)
+
+    table, _ = lax.optimization_barrier((table, near))
+    part, table = lax.optimization_barrier((part, table))
+    lists, starts, tiles = make_lists(table, tile_vals)
+    far = lax.ppermute(near, "half", swap(2))
+    part, far = beside(steps, 1, part, far)
+    self_term = both[rows:]
+
+
+    (away,) = tile_sums(0, 1, lists, starts, near, far, tiles, jnp.bfloat16)
+    came_late = lax.ppermute(away, "core", swap(2))
+    near, _ = lax.optimization_barrier((near, away))
+    (away,) = tile_sums(1, 1, lists, starts, near, far, tiles, jnp.bfloat16)
+    came_early = lax.ppermute(away, "core", swap(2))
+    late, early = tile_sums(2, 2, lists, starts, near, far, tiles, jnp.float32)
     late = under(late + wide(came_late), (2, 2, 2, 4, 2))
     came_late = lax.ppermute(half16(late[1]), "pair", swap(2))
     early = under(early + wide(came_early), (2, 2, 2, 4, 2))

time: 75.1 us -> 71.1 us (0.947)
  the two profiles are of different devices: /device:TPU:32 before, /device:TPU:1 now
where the time goes in v4:
time: 71.1 us; the launch traced here: 70.9 us
  starting transfers between devices  40.7 us (57%)
  waiting for transfers between devices  15.5 us (22%)
  Pallas kernels  5.23 us (7%)
  other arithmetic  4.62 us (6%)
  matrix products  1.89 us (3%)
  between operations  1.71 us (2%)
  local copies, waits for them, and re-layouts  1.26 us (2%)
    ppermute x5, waiting for transfers between devices, join(): lax.ppermute(part, axis, [(i, i ^ k) for i in range(lax.axis_size(axis))])  15.4 us
    ppermute x3, starting transfers between devices, on_device(): came = [lax.ppermute(rounded[:, k], 'z', turn(2 * k, 8)) for k in (1, 3, 2)]  6.66 us
    ppermute x2, starting transfers between devices, on_device(): came_odd = lax.ppermute(odd_ones, 'z', ODD_PAIRS)  5.95 us
    ppermute x5, starting transfers between devices, join(): lax.ppermute(part, axis, [(i, i ^ k) for i in range(lax.axis_size(axis))])  5.67 us
    ppermute x1, starting transfers between devices, on_device(): other = lax.ppermute(part, 'core', swap(2))  5.64 us
    ppermute x3, starting transfers between devices, on_device(): hidden = [lax.ppermute(delta, 'x', turn(k, 4)) for k in (2, 3, 1)]  5.12 us
    ppermute x1, starting transfers between devices, on_device(): far = lax.ppermute(near, 'half', swap(2))  3 us
    ppermute x2, starting transfers between devices, on_device(): came_even = lax.ppermute(even, 'z', EVEN_PAIRS)  2.97 us
  transfers between devices with their start and end apart: 22, of which 4 were waited for; matrix products, arithmetic and copies ran while one was open for 7% of the time, Pallas kernels for 6%

profile of v4, /device:TPU:1, one launch (start us, length us, event | category | flops | bytes accessed | tf_op | source)
XLA Modules:
  0.0 70.9 jit_solution(9319907858029526959)
XLA Ops:
  0.6 0.0 copy-start
  0.7 1.0 %compare_select_fusion = bf16[64,1024]{1,0:T(8,128)(2,1)S(1)} fusion(bf16[64,1024]{1,0:T(8,128)(2,1)} %param.10, bf16[64,1024]{1,0:T(8,128)(2,1)} %param.11), kind=kLoop, calls=%fused_computation.38 | loop fusion | flops 131072 | bytes 393216 | tf_op jit(solution)/shard_map/jit(_where)/select_n | solution.py:197
  1.7 2.1 %collective-permute-start.3 = (bf16[64,1024]{1,0:T(8,128)(2,1)S(1)}, bf16[64,1024]{1,0:T(8,128)(2,1)S(1)}, u32[]{:S(2)}, u32[]{:S(2)}) collective-permute-start(bf16[64,1024]{1,0:T(8,128)(2,1)S(1)} %compare_select_fusion), channel_id=1, source_target_pairs={{0,1},{1,2},{2,3},{3,0},{4,5},{5,6},{6,7},{7,4},{8,9},{9,10},{10,1... | collective-permute-start | bytes 393224 | tf_op jit(solution)/shard_map/ppermute | solution.py:202
  3.8 1.4 %collective-permute-start.2 = (bf16[64,1024]{1,0:T(8,128)(2,1)S(1)}, bf16[64,1024]{1,0:T(8,128)(2,1)S(1)}, u32[]{:S(2)}, u32[]{:S(2)}) collective-permute-start(bf16[64,1024]{1,0:T(8,128)(2,1)S(1)} %compare_select_fusion), channel_id=1, source_target_pairs={{0,3},{1,0},{2,1},{3,2},{4,7},{5,4},{6,5},{7,6},{8,11},{9,8},{10,9... | collective-permute-start | bytes 393224 | tf_op jit(solution)/shard_map/ppermute | solution.py:202
  5.2 1.6 %collective-permute-start.1 = (bf16[64,1024]{1,0:T(8,128)(2,1)S(1)}, bf16[64,1024]{1,0:T(8,128)(2,1)S(1)}, u32[]{:S(2)}, u32[]{:S(2)}) collective-permute-start(bf16[64,1024]{1,0:T(8,128)(2,1)S(1)} %compare_select_fusion), channel_id=1, source_target_pairs={{0,2},{1,3},{2,0},{3,1},{4,6},{5,7},{6,4},{7,5},{8,10},{9,11},{10,... | collective-permute-start | bytes 393224 | tf_op jit(solution)/shard_map/ppermute | solution.py:202
  6.8 0.3 convolution_bitcast_fusion
  7.1 1.3 %convolution_bitcast_fusion.1 = f32[256,64]{0,1:T(8,128)S(1)} fusion(bf16[64,1024]{1,0:T(8,128)(2,1)S(1)} %compare_select_fusion, bf16[256,1024]{1,0:T(8,128)(2,1)} %param.12), kind=kOutput, calls=%fused_computation.6 | convolution fusion | flops 33554432 | bytes 720896 | tf_op jit(solution)/shard_map/dot_general | solution.py:190
  8.5 1.6 %collective-permute-start = (f32[256,64]{0,1:T(8,128)S(1)}, f32[256,64]{0,1:T(8,128)S(1)}, u32[]{:S(2)}, u32[]{:S(2)}) collective-permute-start(f32[256,64]{0,1:T(8,128)S(1)} %fusion.20), channel_id=1, source_target_pairs={{0,8},{8,0},{1,9},{9,1},{2,10},{10,2},{3,11},{11,3},{4,12},{12,4},... | collective-permute-start | bytes 196616 | tf_op jit(solution)/shard_map/ppermute | solution.py:171
  10.7 0.1 add_add_fusion
  10.8 0.1 convert_reduce_fusion.1
  10.9 0.2 convert_reduce_fusion
  11.1 0.1 select_reduce_fusion.1
  11.2 0.1 select_reduce_fusion
  11.3 0.8 %constant_dynamic-slice_fusion = (bf16[64,256]{1,0:T(8,128)(2,1)S(1)}, bf16[64,256]{1,0:T(8,128)(2,1)S(1)}) fusion(bf16[256,256]{1,0:T(8,128)(2,1)} %param.14, s32[]{:T(128)S(6)} %select_n.189, bf16[256,256]{1,0:T(8,128)(2,1)} %param.15), kind=kLoop, calls=%fused_computation.80 | loop fusion | bytes 131076 | tf_op jit(solution)/shard_map/dynamic_slice | solution.py:206
  12.1 0.1 fusion.31
  12.3 0.0 collective-permute-done.2
  12.3 0.3 fusion.3
  12.6 3.0 %collective-permute-start.5 = (bf16[8,64,128]{2,1,0:T(8,128)(2,1)S(1)}, bf16[8,64,128]{2,1,0:T(8,128)(2,1)S(1)}, u32[]{:S(2)}, u32[]{:S(2)}) collective-permute-start(bf16[8,64,128]{2,1,0:T(8,128)(2,1)S(1)} %bitcast_bitcast_fusion.refs_2_), channel_id=1, source_target_pairs={{0,4},{4,0},{1,5},{5,1},{2,6},{6,2},{3,7},{7,3},{8,12},{12,8},{9,1... | collective-permute-start | bytes 393224 | tf_op jit(solution)/shard_map/ppermute | solution.py:229
  15.6 0.1 pad_add_fusion.table_ref
  15.7 1.7 %collective-permute-start.4 = (f32[256,64]{0,1:T(8,128)S(1)}, f32[256,64]{0,1:T(8,128)S(1)}, u32[]{:S(2)}, u32[]{:S(2)}) collective-permute-start(f32[256,64]{0,1:T(8,128)S(1)} %fusion.22), channel_id=1, source_target_pairs={{0,32},{32,0},{64,96},{96,64},{128,160},{160,128},{192,224},{224,1... | collective-permute-start | bytes 196616 | tf_op jit(solution)/shard_map/ppermute | solution.py:176
  17.3 2.5 %shard_map.121 = (s32[320]{0:T(512)S(4)}, s32[4]{0:T(128)S(4)}, bf16[256,128,128]{2,1,0:T(8,128)(2,1)S(1)}) custom-call(s32[521]{0:T(1024)S(1)} %pad_add_fusion.table_ref, bf16[256,128,128]{2,1,0:T(8,128)(2,1)} %vals_ref.1), custom_call_target="tpu_custom_call" | custom-call | bytes 12582912 | tf_op jit(solution)/shard_map/pallas_call | solution.py:81
  19.8 0.0 collective-permute-done.5.refs_3_
  19.8 0.7 %shard_map.122 = bf16[64,64,128]{2,1,0:T(8,128)(2,1)S(1)} custom-call(s32[320]{0:T(512)S(4)} %get-tuple-element.41.refs_0_, s32[4]{0:T(128)S(4)} %get-tuple-element.42.refs_1_, bf16[8,64,128]{2,1,0:T(8,128)(2,1)S(1)} %bitcast_bitcast_fusion.refs_2_, bf16[8,64,128]{2,1,0:T(8,128)(2,1)S(1)} %collective-permute-done.5.refs_3_, ...), custom_call_target="tpu_custom_call" | custom-call | flops 134217728 | bytes 4194304 | tf_op jit(solution)/shard_map/pallas_call | solution.py:131
  20.6 1.7 %collective-permute-start.10 = (bf16[64,64,128]{2,1,0:T(8,128)(2,1)S(1)}, bf16[64,64,128]{2,1,0:T(8,128)(2,1)S(1)}, u32[]{:S(2)}, u32[]{:S(2)}) collective-permute-start(bf16[64,64,128]{2,1,0:T(8,128)(2,1)S(1)} %shard_map.122), channel_id=1, source_target_pairs={{0,8},{8,0},{1,9},{9,1},{2,10},{10,2},{3,11},{11,3},{4,12},{12,4},... | collective-permute-start | bytes 3145736 | tf_op jit(solution)/shard_map/ppermute | solution.py:235
  22.3 0.7 %shard_map.124 = bf16[64,64,128]{2,1,0:T(8,128)(2,1)S(1)} custom-call(s32[320]{0:T(512)S(4)} %get-tuple-element.41.refs_0_, s32[4]{0:T(128)S(4)} %get-tuple-element.42.refs_1_, bf16[8,64,128]{2,1,0:T(8,128)(2,1)S(1)} %bitcast_bitcast_fusion.refs_2_, bf16[8,64,128]{2,1,0:T(8,128)(2,1)S(1)} %collective-permute-done.5.refs_3_, ...), custom_call_target="tpu_custom_call" | custom-call | flops 134217728 | bytes 4194304 | tf_op jit(solution)/shard_map/pallas_call | solution.py:131
  23.0 0.1 collective-permute-start.6
  23.1 1.3 %shard_map.123 = (f32[64,64,128]{2,1,0:T(8,128)S(1)}, f32[64,64,128]{2,1,0:T(8,128)S(1)}) custom-call(s32[320]{0:T(512)S(4)} %get-tuple-element.41.refs_0_, s32[4]{0:T(128)S(4)} %get-tuple-element.42.refs_1_, bf16[8,64,128]{2,1,0:T(8,128)(2,1)S(1)} %bitcast_bitcast_fusion.refs_2_, bf16[8,64,128]{2,1,0:T(8,128)(2,1)S(1)} %collective-permute-done.5.refs_3_, ...), custom_call_target="tpu_custom_call" | custom-call | flops 134217728 | bytes 4194304 | tf_op jit(solution)/shard_map/pallas_call | solution.py:131
  24.4 0.1 collective-permute-done.10
  24.5 0.3 convert_add_fusion
  24.9 0.1 slice.125
  25.0 2.2 %collective-permute-start.11 = (bf16[2,2,4,2,64,128]{5,4,3,2,1,0:T(8,128)(2,1)S(1)}, bf16[2,2,4,2,64,128]{5,4,3,2,1,0:T(8,128)(2,1)S(1)}, u32[]{:S(2)}, u32[]{:S(2)}) collective-permute-start(bf16[2,2,4,2,64,128]{5,4,3,2,1,0:T(8,128)(2,1)S(1)} %bitcast.73), channel_id=1, source_target_pairs={{0,16},{16,0},{1,17},{17,1},{2,18},{18,2},{3,19},{19,3},{4,20},{20... | collective-permute-start | bytes 1572872 | tf_op jit(solution)/shard_map/ppermute | solution.py:241
  27.2 0.4 fusion.53
  27.7 1.2 %collective-permute-start.8 = (bf16[2,4,2,64,128]{4,3,2,1,0:T(8,128)(2,1)S(1)}, bf16[2,4,2,64,128]{4,3,2,1,0:T(8,128)(2,1)S(1)}, u32[]{:S(2)}, u32[]{:S(2)}) collective-permute-start(bf16[2,4,2,64,128]{4,3,2,1,0:T(8,128)(2,1)S(1)} %get-tuple-element.50), channel_id=1, source_target_pairs={{0,32},{32,0},{64,96},{96,64},{128,160},{160,128},{192,224},{224,1... | collective-permute-start | bytes 786440 | tf_op jit(solution)/shard_map/ppermute | solution.py:245
  28.9 4.4 %collective-permute-start.9 = (bf16[2,4,2,64,128]{4,3,2,1,0:T(8,128)(2,1)S(1)}, bf16[2,4,2,64,128]{4,3,2,1,0:T(8,128)(2,1)S(1)}, u32[]{:S(2)}, u32[]{:S(2)}) collective-permute-start(bf16[2,4,2,64,128]{4,3,2,1,0:T(8,128)(2,1)S(1)} %get-tuple-element.51), channel_id=1, source_target_pairs={{0,224},{32,64},{64,32},{96,128},{128,96},{160,192},{192,160},{224... | collective-permute-start | bytes 786440 | tf_op jit(solution)/shard_map/ppermute | solution.py:246
  33.2 1.8 %collective-permute-start.7 = (f32[256,64]{0,1:T(8,128)S(1)}, f32[256,64]{0,1:T(8,128)S(1)}, u32[]{:S(2)}, u32[]{:S(2)}) collective-permute-start(f32[256,64]{0,1:T(8,128)S(1)} %add.262), channel_id=1, source_target_pairs={{0,128},{32,160},{64,192},{96,224},{128,0},{160,32},{192,64},{224,... | collective-permute-start | bytes 196616 | tf_op jit(solution)/shard_map/ppermute | solution.py:176
  35.0 0.1 slice.75
  35.1 0.0 slice-start
  35.1 7.0 %collective-permute-done.7 = f32[256,64]{0,1:T(8,128)S(1)} collective-permute-done((f32[256,64]{0,1:T(8,128)S(1)}, f32[256,64]{0,1:T(8,128)S(1)}, u32[]{:S(2)}, u32[]{:S(2)}) %collective-permute-start.7) | collective-permute-done | bytes 65568 | tf_op jit(solution)/shard_map/ppermute | solution.py:176
  42.1 0.0 collective-permute-done.8
  42.1 0.0 collective-permute-done.9
  42.1 0.2 convert_add_fusion.3
  42.4 0.2 fusion.52
  42.6 0.1 collective-permute-start.13
  42.7 1.8 %collective-permute-start.14 = (bf16[4,2,64,128]{3,2,1,0:T(8,128)(2,1)S(1)}, bf16[4,2,64,128]{3,2,1,0:T(8,128)(2,1)S(1)}, u32[]{:S(2)}, u32[]{:S(2)}) collective-permute-start(bf16[4,2,64,128]{3,2,1,0:T(8,128)(2,1)S(1)} %get-tuple-element.59), channel_id=1, source_target_pairs={{0,32},{32,0},{64,96},{96,64},{128,160},{160,128},{192,224},{224,1... | collective-permute-start | bytes 393224 | tf_op jit(solution)/shard_map/ppermute | solution.py:254
  44.5 1.6 %collective-permute-start.15 = (bf16[4,2,64,128]{3,2,1,0:T(8,128)(2,1)S(1)}, bf16[4,2,64,128]{3,2,1,0:T(8,128)(2,1)S(1)}, u32[]{:S(2)}, u32[]{:S(2)}) collective-permute-start(bf16[4,2,64,128]{3,2,1,0:T(8,128)(2,1)S(1)} %get-tuple-element.60), channel_id=1, source_target_pairs={{0,224},{32,64},{64,32},{96,128},{128,96},{160,192},{192,160},{224... | collective-permute-start | bytes 393224 | tf_op jit(solution)/shard_map/ppermute | solution.py:255
  46.1 0.0 collective-permute-start.12
  46.1 4.6 %collective-permute-done.12 = f32[256,64]{0,1:T(8,128)S(1)} collective-permute-done((f32[256,64]{0,1:T(8,128)S(1)}, f32[256,64]{0,1:T(8,128)S(1)}, u32[]{:S(2)}, u32[]{:S(2)}) %collective-permute-start.12) | collective-permute-done | bytes 65568 | tf_op jit(solution)/shard_map/ppermute | solution.py:176
  50.8 0.0 collective-permute-done.13
  50.8 0.1 fusion.2
  50.8 0.1 fusion.1
  50.9 0.1 fusion
  51.0 1.3 %collective-permute-start.19 = (f32[256,64]{0,1:T(8,128)S(1)}, f32[256,64]{0,1:T(8,128)S(1)}, u32[]{:S(2)}, u32[]{:S(2)}) collective-permute-start(f32[256,64]{0,1:T(8,128)S(1)} %add.268), channel_id=1, source_target_pairs={{0,16},{16,0},{1,17},{17,1},{2,18},{18,2},{3,19},{19,3},{4,20},{20... | collective-permute-start | bytes 196616 | tf_op jit(solution)/shard_map/ppermute | solution.py:176
  52.3 0.1 collective-permute-start.16
  52.4 3.6 %collective-permute-start.17 = (bf16[4,2,64,128]{3,2,1,0:T(8,128)(2,1)S(1)}, bf16[4,2,64,128]{3,2,1,0:T(8,128)(2,1)S(1)}, u32[]{:S(2)}, u32[]{:S(2)}) collective-permute-start(bf16[4,2,64,128]{3,2,1,0:T(8,128)(2,1)S(1)} %get-tuple-element.74), channel_id=1, source_target_pairs={{0,192},{32,224},{64,0},{96,32},{128,64},{160,96},{192,128},{224,1... | collective-permute-start | bytes 393224 | tf_op jit(solution)/shard_map/ppermute | solution.py:263
  55.9 3.0 %collective-permute-start.18 = (bf16[4,2,64,128]{3,2,1,0:T(8,128)(2,1)S(1)}, bf16[4,2,64,128]{3,2,1,0:T(8,128)(2,1)S(1)}, u32[]{:S(2)}, u32[]{:S(2)}) collective-permute-start(bf16[4,2,64,128]{3,2,1,0:T(8,128)(2,1)S(1)} %slice_bitcast_fusion.8), channel_id=1, source_target_pairs={{0,128},{32,160},{64,192},{96,224},{128,0},{160,32},{192,64},{224,... | collective-permute-start | bytes 393224 | tf_op jit(solution)/shard_map/ppermute | solution.py:263
  58.9 0.0 collective-permute-done.19
  59.0 0.9 %collective-permute-start.20 = (f32[256,64]{0,1:T(8,128)S(1)}, f32[256,64]{0,1:T(8,128)S(1)}, u32[]{:S(2)}, u32[]{:S(2)}) collective-permute-start(f32[256,64]{0,1:T(8,128)S(1)} %add.275), channel_id=1, source_target_pairs={{0,4},{4,0},{1,5},{5,1},{2,6},{6,2},{3,7},{7,3},{8,12},{12,8},{9,1... | collective-permute-start | bytes 196616 | tf_op jit(solution)/shard_map/ppermute | solution.py:176
  59.9 3.8 %collective-permute-done.20 = f32[256,64]{0,1:T(8,128)S(1)} collective-permute-done((f32[256,64]{0,1:T(8,128)S(1)}, f32[256,64]{0,1:T(8,128)S(1)}, u32[]{:S(2)}, u32[]{:S(2)}) %collective-permute-start.20) | collective-permute-done | bytes 65568 | tf_op jit(solution)/shard_map/ppermute | solution.py:176
  63.7 5.6 %collective-permute-start.21 = (f32[256,64]{0,1:T(8,128)S(1)}, f32[256,64]{0,1:T(8,128)S(1)}, u32[]{:S(2)}, u32[]{:S(2)}) collective-permute-start(f32[256,64]{0,1:T(8,128)S(1)} %add.276), channel_id=1, source_target_pairs={{0,8},{8,0},{1,9},{9,1},{2,10},{10,2},{3,11},{11,3},{4,12},{12,4},... | collective-permute-start | bytes 196616 | tf_op jit(solution)/shard_map/ppermute | solution.py:265
  69.3 0.0 collective-permute-done.16
  69.3 0.1 fusion.16
  69.4 0.2 copy.29
  69.6 0.7 %fusion.17 = bf16[64,1024]{1,0:T(8,128)(2,1)} fusion(f32[8,8,8,128]{3,2,1,0:T(8,128)S(1)} %bitcast.71, f32[128,1024]{1,0:T(8,128)S(1)} %fusion.3), kind=kLoop, calls=%fused_computation.31 | loop fusion | flops 131072 | bytes 655360 | tf_op jit(solution)/shard_map/convert_element_type | solution.py:152
  70.3 0.7 broadcast_select_fusion
  (34 shorter events, 0.3 us)
Async XLA Ops:
  0.6 6.2 %copy-start = (bf16[256,1024]{1,0:T(8,128)(2,1)S(1)}, bf16[256,1024]{1,0:T(8,128)(2,1)}, u32[]{:S(2)}) copy-start(bf16[256,1024]{1,0:T(8,128)(2,1)} %param.13) | copy-start | bytes 1572868
  0.6 10.1 %copy-start.3 = (s32[256]{0:T(256)S(1)}, s32[256]{0:T(256)}, u32[]{:S(2)}) copy-start(s32[256]{0:T(256)} %param.17) | copy-start | bytes 3076
  0.7 10.1 %copy-start.2 = (s32[256]{0:T(256)S(1)}, s32[256]{0:T(256)}, u32[]{:S(2)}) copy-start(s32[256]{0:T(256)} %param.16) | copy-start | bytes 3076
  1.7 10.5 %collective-permute-start.3 = (bf16[64,1024]{1,0:T(8,128)(2,1)S(1)}, bf16[64,1024]{1,0:T(8,128)(2,1)S(1)}, u32[]{:S(2)}, u32[]{:S(2)}) collective-permute-start(bf16[64,1024]{1,0:T(8,128)(2,1)S(1)} %compare_select_fusion), channel_id=1, source_target_pairs={{0,1},{1,2},{2,3},{3,0},{4,5},{5,6},{6,7},{7,4},{8,9},{9,10},{10,1... | collective-permute-start | bytes 393224 | tf_op jit(solution)/shard_map/ppermute | solution.py:202
  3.8 8.4 %collective-permute-start.2 = (bf16[64,1024]{1,0:T(8,128)(2,1)S(1)}, bf16[64,1024]{1,0:T(8,128)(2,1)S(1)}, u32[]{:S(2)}, u32[]{:S(2)}) collective-permute-start(bf16[64,1024]{1,0:T(8,128)(2,1)S(1)} %compare_select_fusion), channel_id=1, source_target_pairs={{0,3},{1,0},{2,1},{3,2},{4,7},{5,4},{6,5},{7,6},{8,11},{9,8},{10,9... | collective-permute-start | bytes 393224 | tf_op jit(solution)/shard_map/ppermute | solution.py:202
  5.2 7.1 %collective-permute-start.1 = (bf16[64,1024]{1,0:T(8,128)(2,1)S(1)}, bf16[64,1024]{1,0:T(8,128)(2,1)S(1)}, u32[]{:S(2)}, u32[]{:S(2)}) collective-permute-start(bf16[64,1024]{1,0:T(8,128)(2,1)S(1)} %compare_select_fusion), channel_id=1, source_target_pairs={{0,2},{1,3},{2,0},{3,1},{4,6},{5,7},{6,4},{7,5},{8,10},{9,11},{10,... | collective-permute-start | bytes 393224 | tf_op jit(solution)/shard_map/ppermute | solution.py:202
  8.5 3.7 %collective-permute-start = (f32[256,64]{0,1:T(8,128)S(1)}, f32[256,64]{0,1:T(8,128)S(1)}, u32[]{:S(2)}, u32[]{:S(2)}) collective-permute-start(f32[256,64]{0,1:T(8,128)S(1)} %fusion.20), channel_id=1, source_target_pairs={{0,8},{8,0},{1,9},{9,1},{2,10},{10,2},{3,11},{11,3},{4,12},{12,4},... | collective-permute-start | bytes 196616 | tf_op jit(solution)/shard_map/ppermute | solution.py:171
  12.6 7.2 %collective-permute-start.5 = (bf16[8,64,128]{2,1,0:T(8,128)(2,1)S(1)}, bf16[8,64,128]{2,1,0:T(8,128)(2,1)S(1)}, u32[]{:S(2)}, u32[]{:S(2)}) collective-permute-start(bf16[8,64,128]{2,1,0:T(8,128)(2,1)S(1)} %bitcast_bitcast_fusion.refs_2_), channel_id=1, source_target_pairs={{0,4},{4,0},{1,5},{5,1},{2,6},{6,2},{3,7},{7,3},{8,12},{12,8},{9,1... | collective-permute-start | bytes 393224 | tf_op jit(solution)/shard_map/ppermute | solution.py:229
  15.7 4.1 %collective-permute-start.4 = (f32[256,64]{0,1:T(8,128)S(1)}, f32[256,64]{0,1:T(8,128)S(1)}, u32[]{:S(2)}, u32[]{:S(2)}) collective-permute-start(f32[256,64]{0,1:T(8,128)S(1)} %fusion.22), channel_id=1, source_target_pairs={{0,32},{32,0},{64,96},{96,64},{128,160},{160,128},{192,224},{224,1... | collective-permute-start | bytes 196616 | tf_op jit(solution)/shard_map/ppermute | solution.py:176
  20.6 4.0 %collective-permute-start.10 = (bf16[64,64,128]{2,1,0:T(8,128)(2,1)S(1)}, bf16[64,64,128]{2,1,0:T(8,128)(2,1)S(1)}, u32[]{:S(2)}, u32[]{:S(2)}) collective-permute-start(bf16[64,64,128]{2,1,0:T(8,128)(2,1)S(1)} %shard_map.122), channel_id=1, source_target_pairs={{0,8},{8,0},{1,9},{9,1},{2,10},{10,2},{3,11},{11,3},{4,12},{12,4},... | collective-permute-start | bytes 3145736 | tf_op jit(solution)/shard_map/ppermute | solution.py:235
  23.0 4.2 %collective-permute-start.6 = (bf16[64,64,128]{2,1,0:T(8,128)(2,1)S(1)}, bf16[64,64,128]{2,1,0:T(8,128)(2,1)S(1)}, u32[]{:S(2)}, u32[]{:S(2)}) collective-permute-start(bf16[64,64,128]{2,1,0:T(8,128)(2,1)S(1)} %shard_map.124), channel_id=1, source_target_pairs={{0,8},{8,0},{1,9},{9,1},{2,10},{10,2},{3,11},{11,3},{4,12},{12,4},... | collective-permute-start | bytes 3145736 | tf_op jit(solution)/shard_map/ppermute | solution.py:238
  24.9 10.2 %copy-start.1 = (f32[64,64,128]{2,1,0:T(8,128)}, f32[64,64,128]{2,1,0:T(8,128)S(1)}, u32[]{:S(2)}) copy-start(f32[64,64,128]{2,1,0:T(8,128)S(1)} %convert_add_fusion) | copy-start | bytes 6291460
  25.0 17.2 %collective-permute-start.11 = (bf16[2,2,4,2,64,128]{5,4,3,2,1,0:T(8,128)(2,1)S(1)}, bf16[2,2,4,2,64,128]{5,4,3,2,1,0:T(8,128)(2,1)S(1)}, u32[]{:S(2)}, u32[]{:S(2)}) collective-permute-start(bf16[2,2,4,2,64,128]{5,4,3,2,1,0:T(8,128)(2,1)S(1)} %bitcast.73), channel_id=1, source_target_pairs={{0,16},{16,0},{1,17},{17,1},{2,18},{18,2},{3,19},{19,3},{4,20},{20... | collective-permute-start | bytes 1572872 | tf_op jit(solution)/shard_map/ppermute | solution.py:241
  27.7 14.5 %collective-permute-start.8 = (bf16[2,4,2,64,128]{4,3,2,1,0:T(8,128)(2,1)S(1)}, bf16[2,4,2,64,128]{4,3,2,1,0:T(8,128)(2,1)S(1)}, u32[]{:S(2)}, u32[]{:S(2)}) collective-permute-start(bf16[2,4,2,64,128]{4,3,2,1,0:T(8,128)(2,1)S(1)} %get-tuple-element.50), channel_id=1, source_target_pairs={{0,32},{32,0},{64,96},{96,64},{128,160},{160,128},{192,224},{224,1... | collective-permute-start | bytes 786440 | tf_op jit(solution)/shard_map/ppermute | solution.py:245
  28.9 13.3 %collective-permute-start.9 = (bf16[2,4,2,64,128]{4,3,2,1,0:T(8,128)(2,1)S(1)}, bf16[2,4,2,64,128]{4,3,2,1,0:T(8,128)(2,1)S(1)}, u32[]{:S(2)}, u32[]{:S(2)}) collective-permute-start(bf16[2,4,2,64,128]{4,3,2,1,0:T(8,128)(2,1)S(1)} %get-tuple-element.51), channel_id=1, source_target_pairs={{0,224},{32,64},{64,32},{96,128},{128,96},{160,192},{192,160},{224... | collective-permute-start | bytes 786440 | tf_op jit(solution)/shard_map/ppermute | solution.py:246
  33.2 8.9 %collective-permute-start.7 = (f32[256,64]{0,1:T(8,128)S(1)}, f32[256,64]{0,1:T(8,128)S(1)}, u32[]{:S(2)}, u32[]{:S(2)}) collective-permute-start(f32[256,64]{0,1:T(8,128)S(1)} %add.262), channel_id=1, source_target_pairs={{0,128},{32,160},{64,192},{96,224},{128,0},{160,32},{192,64},{224,... | collective-permute-start | bytes 196616 | tf_op jit(solution)/shard_map/ppermute | solution.py:176
  35.1 7.3 %slice-start = ((f32[64,64,128]{2,1,0:T(8,128)}), f32[32,64,128]{2,1,0:T(8,128)S(1)}, s32[]{:S(2)}) async-start(f32[64,64,128]{2,1,0:T(8,128)} %copy-done.1), calls=%async_computation | async-start | bytes 2097152 | tf_op jit(solution)/shard_map/slice | solution.py:250
  42.6 8.1 %collective-permute-start.13 = (bf16[2,4,2,64,128]{4,3,2,1,0:T(8,128)(2,1)S(1)}, bf16[2,4,2,64,128]{4,3,2,1,0:T(8,128)(2,1)S(1)}, u32[]{:S(2)}, u32[]{:S(2)}) collective-permute-start(bf16[2,4,2,64,128]{4,3,2,1,0:T(8,128)(2,1)S(1)} %fusion.11), channel_id=1, source_target_pairs={{0,16},{16,0},{1,17},{17,1},{2,18},{18,2},{3,19},{19,3},{4,20},{20... | collective-permute-start | bytes 786440 | tf_op jit(solution)/shard_map/ppermute | solution.py:253
  42.7 8.0 %collective-permute-start.14 = (bf16[4,2,64,128]{3,2,1,0:T(8,128)(2,1)S(1)}, bf16[4,2,64,128]{3,2,1,0:T(8,128)(2,1)S(1)}, u32[]{:S(2)}, u32[]{:S(2)}) collective-permute-start(bf16[4,2,64,128]{3,2,1,0:T(8,128)(2,1)S(1)} %get-tuple-element.59), channel_id=1, source_target_pairs={{0,32},{32,0},{64,96},{96,64},{128,160},{160,128},{192,224},{224,1... | collective-permute-start | bytes 393224 | tf_op jit(solution)/shard_map/ppermute | solution.py:254
  44.5 6.2 %collective-permute-start.15 = (bf16[4,2,64,128]{3,2,1,0:T(8,128)(2,1)S(1)}, bf16[4,2,64,128]{3,2,1,0:T(8,128)(2,1)S(1)}, u32[]{:S(2)}, u32[]{:S(2)}) collective-permute-start(bf16[4,2,64,128]{3,2,1,0:T(8,128)(2,1)S(1)} %get-tuple-element.60), channel_id=1, source_target_pairs={{0,224},{32,64},{64,32},{96,128},{128,96},{160,192},{192,160},{224... | collective-permute-start | bytes 393224 | tf_op jit(solution)/shard_map/ppermute | solution.py:255
  46.1 4.6 %collective-permute-start.12 = (f32[256,64]{0,1:T(8,128)S(1)}, f32[256,64]{0,1:T(8,128)S(1)}, u32[]{:S(2)}, u32[]{:S(2)}) collective-permute-start(f32[256,64]{0,1:T(8,128)S(1)} %add.264), channel_id=1, source_target_pairs={{0,64},{32,96},{64,0},{96,32},{128,192},{160,224},{192,128},{224,1... | collective-permute-start | bytes 196616 | tf_op jit(solution)/shard_map/ppermute | solution.py:176
  51.0 8.0 %collective-permute-start.19 = (f32[256,64]{0,1:T(8,128)S(1)}, f32[256,64]{0,1:T(8,128)S(1)}, u32[]{:S(2)}, u32[]{:S(2)}) collective-permute-start(f32[256,64]{0,1:T(8,128)S(1)} %add.268), channel_id=1, source_target_pairs={{0,16},{16,0},{1,17},{17,1},{2,18},{18,2},{3,19},{19,3},{4,20},{20... | collective-permute-start | bytes 196616 | tf_op jit(solution)/shard_map/ppermute | solution.py:176
  52.3 17.0 %collective-permute-start.16 = (bf16[4,2,64,128]{3,2,1,0:T(8,128)(2,1)S(1)}, bf16[4,2,64,128]{3,2,1,0:T(8,128)(2,1)S(1)}, u32[]{:S(2)}, u32[]{:S(2)}) collective-permute-start(bf16[4,2,64,128]{3,2,1,0:T(8,128)(2,1)S(1)} %get-tuple-element.73), channel_id=1, source_target_pairs={{0,64},{32,96},{64,128},{96,160},{128,192},{160,224},{192,0},{224,... | collective-permute-start | bytes 393224 | tf_op jit(solution)/shard_map/ppermute | solution.py:263
  52.4 17.0 %collective-permute-start.17 = (bf16[4,2,64,128]{3,2,1,0:T(8,128)(2,1)S(1)}, bf16[4,2,64,128]{3,2,1,0:T(8,128)(2,1)S(1)}, u32[]{:S(2)}, u32[]{:S(2)}) collective-permute-start(bf16[4,2,64,128]{3,2,1,0:T(8,128)(2,1)S(1)} %get-tuple-element.74), channel_id=1, source_target_pairs={{0,192},{32,224},{64,0},{96,32},{128,64},{160,96},{192,128},{224,1... | collective-permute-start | bytes 393224 | tf_op jit(solution)/shard_map/ppermute | solution.py:263
  55.9 13.4 %collective-permute-start.18 = (bf16[4,2,64,128]{3,2,1,0:T(8,128)(2,1)S(1)}, bf16[4,2,64,128]{3,2,1,0:T(8,128)(2,1)S(1)}, u32[]{:S(2)}, u32[]{:S(2)}) collective-permute-start(bf16[4,2,64,128]{3,2,1,0:T(8,128)(2,1)S(1)} %slice_bitcast_fusion.8), channel_id=1, source_target_pairs={{0,128},{32,160},{64,192},{96,224},{128,0},{160,32},{192,64},{224,... | collective-permute-start | bytes 393224 | tf_op jit(solution)/shard_map/ppermute | solution.py:263
  59.0 4.7 %collective-permute-start.20 = (f32[256,64]{0,1:T(8,128)S(1)}, f32[256,64]{0,1:T(8,128)S(1)}, u32[]{:S(2)}, u32[]{:S(2)}) collective-permute-start(f32[256,64]{0,1:T(8,128)S(1)} %add.275), channel_id=1, source_target_pairs={{0,4},{4,0},{1,5},{5,1},{2,6},{6,2},{3,7},{7,3},{8,12},{12,8},{9,1... | collective-permute-start | bytes 196616 | tf_op jit(solution)/shard_map/ppermute | solution.py:176
  63.7 6.6 %collective-permute-start.21 = (f32[256,64]{0,1:T(8,128)S(1)}, f32[256,64]{0,1:T(8,128)S(1)}, u32[]{:S(2)}, u32[]{:S(2)}) collective-permute-start(f32[256,64]{0,1:T(8,128)S(1)} %add.276), channel_id=1, source_target_pairs={{0,8},{8,0},{1,9},{9,1},{2,10},{10,2},{3,11},{11,3},{4,12},{12,4},... | collective-permute-start | bytes 196616 | tf_op jit(solution)/shard_map/ppermute | solution.py:265
